TPU v7x, 512 devices: a whole 4x4x16 slice. The times are simulated.
512 devices in a mesh: frames: 128 (over z, y, core), heads: 4 (over x).
Axes of the slice: x: 4, y: 4, z: 16, core: 2. Of those that a mesh axis runs over, the one named last changes fastest.
Arguments:
- queries: bfloat16 [32768, 1536], P(('frames', 'heads')), may hold values from -6 to 6
- keys: bfloat16 [32768, 1536], P(('frames', 'heads')), may hold values from -12 to 12
- values: bfloat16 [32768, 1536], P(('frames', 'heads')), may hold values from -24 to 24
- block_picks: int32 [128, 128, 2], replicated, may hold values from 0 to 1, as said below
- block_counts: int32 [128, 128], replicated, may hold values from 0 to 2, as said below
Outputs:
- attended: bfloat16 [32768, 1536], P(('frames', 'heads'))
Inputs may be any that keep to these rules, and one draw needn't show every extreme that they name: block_picks[g, h, :] are 2 distinct block numbers. block_counts[g, h] is 2 where |g - h| = 1, and 0 where |g - h| is not a power of two.
All inputs are finite; a program needn't handle non-finite values.
Results may differ from a plain program's by a relative error of at most 0.0065.
Values may be sent and summed in bfloat16 or wider, within the bound.
A program may use at most 64 MiB of HBM per device.

v0:
```python
import math

import jax
import jax.numpy as jnp
from jax import lax
from jax.sharding import PartitionSpec as P

HEAD_DIM = 128
BLOCK = 128


def shifted(block, axis, distance):
    devices = range(lax.axis_size(axis))
    route = [(i - distance, i) for i in devices if i - distance in devices]
    return lax.ppermute(block, axis, route)


def attend_tile(running, query_heads, key_rows, value_rows, live_mask, score_scale):
    maximum, row_total, accumulated = running
    head_count = query_heads.shape[1]
    key_heads = key_rows.reshape(key_rows.shape[0], head_count, -1)
    value_heads = value_rows.reshape(value_rows.shape[0], head_count, -1)
    scores = (
        jnp.einsum("qhd,khd->hqk", query_heads, key_heads, preferred_element_type=jnp.float32)
        * score_scale
    )
    masked = jnp.where(live_mask[None, None, :], scores, -jnp.inf)
    newest = jnp.maximum(maximum, jnp.max(masked, axis=2))
    rescale = jnp.exp(maximum - newest)
    weights = jnp.where(live_mask[None, None, :], jnp.exp(scores - newest[:, :, None]), 0.0)
    row_total = row_total * rescale + jnp.sum(weights, axis=2)
    partial_out = jnp.einsum(
        "hqk,khd->qhd",
        weights.astype(jnp.bfloat16),
        value_heads,
        preferred_element_type=jnp.float32,
    )
    accumulated = accumulated * jnp.transpose(rescale)[:, :, None] + partial_out
    return (newest, row_total, accumulated)


def local(queries, keys, values, block_picks, block_counts):
    head_q, head_k, head_v = (
        lax.all_to_all(queries, "heads", split_axis=1, concat_axis=0, tiled=True),
        lax.all_to_all(keys, "heads", split_axis=1, concat_axis=0, tiled=True),
        lax.all_to_all(values, "heads", split_axis=1, concat_axis=0, tiled=True),
    )
    group_len = head_q.shape[0]
    columns = head_q.shape[1]
    head_count = columns // HEAD_DIM
    block_count = group_len // BLOCK
    pick_count = block_picks.shape[2]
    own_group = lax.axis_index("frames")
    group_total = lax.axis_size("frames")
    score_scale = 1.0 / math.sqrt(HEAD_DIM)
    query_heads = head_q.reshape(group_len, head_count, HEAD_DIM)
    slot_block = jnp.arange(pick_count * BLOCK, dtype=jnp.int32) // BLOCK
    running = (
        jnp.full((head_count, group_len), -jnp.inf, jnp.float32),
        jnp.zeros((head_count, group_len), jnp.float32),
        jnp.zeros((group_len, head_count, HEAD_DIM), jnp.float32),
    )
    everyone = jnp.ones((group_len,), dtype=bool)
    running = attend_tile(running, query_heads, head_k, head_v, everyone, score_scale)

    def visit(current, offset):
        source = own_group - offset
        inside = (source >= 0) & (source < group_total)
        source_row = jnp.clip(source, 0, group_total - 1)
        live_count = jnp.where(inside, block_counts[own_group, source_row], 0)
        far_keys, far_values = shifted((head_k, head_v), "frames", offset)
        chosen = block_picks[own_group, source_row]
        got_keys = jnp.take(far_keys.reshape(block_count, BLOCK, columns), chosen, axis=0).reshape(
            pick_count * BLOCK, columns
        )
        got_values = jnp.take(
            far_values.reshape(block_count, BLOCK, columns), chosen, axis=0
        ).reshape(pick_count * BLOCK, columns)
        live_mask = slot_block < live_count
        return attend_tile(current, query_heads, got_keys, got_values, live_mask, score_scale)

    for exponent in range(group_total.bit_length()):
        distance = 2**exponent
        if distance < group_total:
            running = visit(running, distance)
            running = visit(running, -distance)
    maximum, row_total, accumulated = running
    mixed = accumulated / jnp.transpose(row_total)[:, :, None]
    attended_heads = mixed.reshape(group_len, columns).astype(jnp.bfloat16)
    return lax.all_to_all(attended_heads, "heads", split_axis=0, concat_axis=1, tiled=True)


def solution(mesh):
    placed = (
        P(("frames", "heads"), None),
        P(("frames", "heads"), None),
        P(("frames", "heads"), None),
        P(),
        P(),
    )
    return jax.shard_map(
        local, mesh=mesh, in_specs=placed, out_specs=P(("frames", "heads"), None), check_vma=False
    )
```

profile of v0, /device:TPU:152, one launch (start us, length us, event | category | flops | bytes accessed | tf_op | source)
XLA Modules:
  0.0 326.8 jit_solution(2289418867812417003)
XLA Ops:
  1.6 4.3 %all-to-all-start.1 = ((bf16[64,4,384]{2,0,1:T(8,128)(2,1)}), bf16[64,4,384]{2,0,1:T(8,128)(2,1)S(1)}, u32[]{:S(2)}, u32[]{:S(2)}) async-start(bf16[64,4,384]{2,0,1:T(8,128)(2,1)} %bitcast.482), calls=%async_computation.1 | async-start | bytes 393216 | tf_op jit(solution)/shard_map/all_to_all | solution.py:45
  30.9 4.9 %all-to-all-start.2 = ((bf16[64,4,384]{2,0,1:T(8,128)(2,1)}), bf16[64,4,384]{2,0,1:T(8,128)(2,1)}, u32[]{:S(2)}, u32[]{:S(2)}) async-start(bf16[64,4,384]{2,0,1:T(8,128)(2,1)} %bitcast.481), calls=%async_computation.2 | async-start | bytes 393216 | tf_op jit(solution)/shard_map/all_to_all | solution.py:46
  38.9 3.4 %all-to-all-done.2 = bf16[64,4,384]{2,0,1:T(8,128)(2,1)} async-done(((bf16[64,4,384]{2,0,1:T(8,128)(2,1)}), bf16[64,4,384]{2,0,1:T(8,128)(2,1)}, u32[]{:S(2)}, u32[]{:S(2)}) %all-to-all-start.2) | async-done | bytes 196640 | tf_op jit(solution)/shard_map/all_to_all | solution.py:46
  42.2 3.4 %all-to-all-start = ((bf16[64,4,384]{2,0,1:T(8,128)(2,1)}), bf16[64,4,384]{2,0,1:T(8,128)(2,1)S(1)}, u32[]{:S(2)}, u32[]{:S(2)}) async-start(bf16[64,4,384]{2,0,1:T(8,128)(2,1)} %bitcast.483), calls=%async_computation | async-start | bytes 393216 | tf_op jit(solution)/shard_map/all_to_all | solution.py:44
  48.7 5.2 %collective-permute-start.16 = (bf16[256,384]{1,0:T(8,128)(2,1)S(1)}, bf16[256,384]{1,0:T(8,128)(2,1)S(1)}, u32[]{:S(2)}, u32[]{:S(2)}) collective-permute-start(bf16[256,384]{1,0:T(8,128)(2,1)S(1)} %bitcast.485), channel_id=1, source_target_pairs={{0,64},{4,68},{8,72},{12,76},{16,80},{20,84},{24,88},{28,92},{32,9... | collective-permute-start | bytes 589832 | tf_op jit(solution)/shard_map/ppermute | solution.py:15
  53.9 2.8 collective-permute-start.19
  56.7 5.5 %collective-permute-start.17 = (bf16[256,384]{1,0:T(8,128)(2,1)}, bf16[256,384]{1,0:T(8,128)(2,1)S(1)}, u32[]{:S(2)}, u32[]{:S(2)}) collective-permute-start(bf16[256,384]{1,0:T(8,128)(2,1)} %bitcast.9), channel_id=1, source_target_pairs={{0,64},{4,68},{8,72},{12,76},{16,80},{20,84},{24,88},{28,92},{32,9... | collective-permute-start | bytes 589832 | tf_op jit(solution)/shard_map/ppermute | solution.py:15
  62.2 2.9 collective-permute-start.14
  69.3 4.0 %collective-permute-start.12 = (bf16[256,384]{1,0:T(8,128)(2,1)S(1)}, bf16[256,384]{1,0:T(8,128)(2,1)S(1)}, u32[]{:S(2)}, u32[]{:S(2)}) collective-permute-start(bf16[256,384]{1,0:T(8,128)(2,1)S(1)} %bitcast.488), channel_id=1, source_target_pairs={{0,32},{4,36},{8,40},{12,44},{16,48},{20,52},{24,56},{28,60},{32,6... | collective-permute-start | bytes 589832 | tf_op jit(solution)/shard_map/ppermute | solution.py:15
  74.8 3.5 %collective-permute-start.13 = (bf16[256,384]{1,0:T(8,128)(2,1)}, bf16[256,384]{1,0:T(8,128)(2,1)}, u32[]{:S(2)}, u32[]{:S(2)}) collective-permute-start(bf16[256,384]{1,0:T(8,128)(2,1)} %bitcast.9), channel_id=1, source_target_pairs={{0,32},{4,36},{8,40},{12,44},{16,48},{20,52},{24,56},{28,60},{32,6... | collective-permute-start | bytes 589832 | tf_op jit(solution)/shard_map/ppermute | solution.py:15
  78.9 3.1 collective-permute-start.10
  83.5 5.3 %collective-permute-start.11 = (bf16[256,384]{1,0:T(8,128)(2,1)}, bf16[256,384]{1,0:T(8,128)(2,1)}, u32[]{:S(2)}, u32[]{:S(2)}) collective-permute-start(bf16[256,384]{1,0:T(8,128)(2,1)} %bitcast.9), channel_id=1, source_target_pairs={{16,0},{20,4},{24,8},{28,12},{32,16},{36,20},{40,24},{44,28},{48,3... | collective-permute-start | bytes 589832 | tf_op jit(solution)/shard_map/ppermute | solution.py:15
  89.4 3.0 collective-permute-start.8
  93.8 4.2 %collective-permute-start.9 = (bf16[256,384]{1,0:T(8,128)(2,1)}, bf16[256,384]{1,0:T(8,128)(2,1)S(1)}, u32[]{:S(2)}, u32[]{:S(2)}) collective-permute-start(bf16[256,384]{1,0:T(8,128)(2,1)} %bitcast.9), channel_id=1, source_target_pairs={{0,16},{4,20},{8,24},{12,28},{16,32},{20,36},{24,40},{28,44},{32,4... | collective-permute-start | bytes 589832 | tf_op jit(solution)/shard_map/ppermute | solution.py:15
  106.9 5.6 %collective-permute-start.4 = (bf16[256,384]{1,0:T(8,128)(2,1)S(1)}, bf16[256,384]{1,0:T(8,128)(2,1)}, u32[]{:S(2)}, u32[]{:S(2)}) collective-permute-start(bf16[256,384]{1,0:T(8,128)(2,1)S(1)} %bitcast.492), channel_id=1, source_target_pairs={{0,8},{4,12},{8,16},{12,20},{16,24},{20,28},{24,32},{28,36},{32,40... | collective-permute-start | bytes 589832 | tf_op jit(solution)/shard_map/ppermute | solution.py:15
  115.0 3.2 collective-permute-start.5
  123.4 2.8 collective-permute-start.3
  133.9 5.4 %collective-permute-start.1 = (bf16[256,384]{1,0:T(8,128)(2,1)}, bf16[256,384]{1,0:T(8,128)(2,1)}, u32[]{:S(2)}, u32[]{:S(2)}) collective-permute-start(bf16[256,384]{1,0:T(8,128)(2,1)} %bitcast.9), channel_id=1, source_target_pairs={{0,4},{4,8},{8,12},{12,16},{16,20},{20,24},{24,28},{28,32},{32,36}... | collective-permute-start | bytes 589832 | tf_op jit(solution)/shard_map/ppermute | solution.py:15
  141.0 11.6 %collective-permute-start.24 = (bf16[256,384]{1,0:T(8,128)(2,1)S(1)}, bf16[256,384]{1,0:T(8,128)(2,1)}, u32[]{:S(2)}, u32[]{:S(2)}) collective-permute-start(bf16[256,384]{1,0:T(8,128)(2,1)S(1)} %bitcast.495), channel_id=1, source_target_pairs={{0,256},{4,260},{8,264},{12,268},{16,272},{20,276},{24,280},{28,28... | collective-permute-start | bytes 589832 | tf_op jit(solution)/shard_map/ppermute | solution.py:15
  161.9 3.3 %collective-permute-start.22 = (bf16[256,384]{1,0:T(8,128)(2,1)S(1)}, bf16[256,384]{1,0:T(8,128)(2,1)}, u32[]{:S(2)}, u32[]{:S(2)}) collective-permute-start(bf16[256,384]{1,0:T(8,128)(2,1)S(1)} %bitcast.496), channel_id=1, source_target_pairs={{128,0},{132,4},{136,8},{140,12},{144,16},{148,20},{152,24},{156,2... | collective-permute-start | bytes 589832 | tf_op jit(solution)/shard_map/ppermute | solution.py:15
  175.4 7.8 %collective-permute-start.20 = (bf16[256,384]{1,0:T(8,128)(2,1)S(1)}, bf16[256,384]{1,0:T(8,128)(2,1)}, u32[]{:S(2)}, u32[]{:S(2)}) collective-permute-start(bf16[256,384]{1,0:T(8,128)(2,1)S(1)} %bitcast.497), channel_id=1, source_target_pairs={{0,128},{4,132},{8,136},{12,140},{16,144},{20,148},{24,152},{28,15... | collective-permute-start | bytes 589832 | tf_op jit(solution)/shard_map/ppermute | solution.py:15
  189.1 7.0 %collective-permute-start.21 = (bf16[256,384]{1,0:T(8,128)(2,1)}, bf16[256,384]{1,0:T(8,128)(2,1)}, u32[]{:S(2)}, u32[]{:S(2)}) collective-permute-start(bf16[256,384]{1,0:T(8,128)(2,1)} %bitcast.9), channel_id=1, source_target_pairs={{0,128},{4,132},{8,136},{12,140},{16,144},{20,148},{24,152},{28,15... | collective-permute-start | bytes 589832 | tf_op jit(solution)/shard_map/ppermute | solution.py:15
  223.4 25.0 %collective-permute-done.26 = bf16[256,384]{1,0:T(8,128)(2,1)} collective-permute-done((bf16[256,384]{1,0:T(8,128)(2,1)S(1)}, bf16[256,384]{1,0:T(8,128)(2,1)}, u32[]{:S(2)}, u32[]{:S(2)}) %collective-permute-start.26) | collective-permute-done | bytes 196640 | tf_op jit(solution)/shard_map/ppermute | solution.py:15
  315.2 10.9 %all_to_all.70 = bf16[4,64,384]{2,1,0:T(8,128)(2,1)S(1)} all-to-all(bf16[4,64,384]{2,1,0:T(8,128)(2,1)S(1)} %convert_element_type.68), channel_id=1, replica_groups=mesh['frames'=128,'heads'=4] {'heads'}, dimensions={0} | all-to-all | bytes 393216 | tf_op jit(solution)/shard_map/all_to_all | solution.py:90
  (314 shorter events, 179.1 us)
Async XLA Ops:
  1.6 29.3 %all-to-all-start.1 = ((bf16[64,4,384]{2,0,1:T(8,128)(2,1)}), bf16[64,4,384]{2,0,1:T(8,128)(2,1)S(1)}, u32[]{:S(2)}, u32[]{:S(2)}) async-start(bf16[64,4,384]{2,0,1:T(8,128)(2,1)} %bitcast.482), calls=%async_computation.1 | async-start | bytes 393216 | tf_op jit(solution)/shard_map/all_to_all | solution.py:45
  48.7 26.0 %collective-permute-start.16 = (bf16[256,384]{1,0:T(8,128)(2,1)S(1)}, bf16[256,384]{1,0:T(8,128)(2,1)S(1)}, u32[]{:S(2)}, u32[]{:S(2)}) collective-permute-start(bf16[256,384]{1,0:T(8,128)(2,1)S(1)} %bitcast.485), channel_id=1, source_target_pairs={{0,64},{4,68},{8,72},{12,76},{16,80},{20,84},{24,88},{28,92},{32,9... | collective-permute-start | bytes 589832 | tf_op jit(solution)/shard_map/ppermute | solution.py:15
  69.3 24.5 %collective-permute-start.12 = (bf16[256,384]{1,0:T(8,128)(2,1)S(1)}, bf16[256,384]{1,0:T(8,128)(2,1)S(1)}, u32[]{:S(2)}, u32[]{:S(2)}) collective-permute-start(bf16[256,384]{1,0:T(8,128)(2,1)S(1)} %bitcast.488), channel_id=1, source_target_pairs={{0,32},{4,36},{8,40},{12,44},{16,48},{20,52},{24,56},{28,60},{32,6... | collective-permute-start | bytes 589832 | tf_op jit(solution)/shard_map/ppermute | solution.py:15
  74.8 23.9 %collective-permute-start.13 = (bf16[256,384]{1,0:T(8,128)(2,1)}, bf16[256,384]{1,0:T(8,128)(2,1)}, u32[]{:S(2)}, u32[]{:S(2)}) collective-permute-start(bf16[256,384]{1,0:T(8,128)(2,1)} %bitcast.9), channel_id=1, source_target_pairs={{0,32},{4,36},{8,40},{12,44},{16,48},{20,52},{24,56},{28,60},{32,6... | collective-permute-start | bytes 589832 | tf_op jit(solution)/shard_map/ppermute | solution.py:15
  78.9 24.9 %collective-permute-start.10 = (bf16[256,384]{1,0:T(8,128)(2,1)S(1)}, bf16[256,384]{1,0:T(8,128)(2,1)S(1)}, u32[]{:S(2)}, u32[]{:S(2)}) collective-permute-start(bf16[256,384]{1,0:T(8,128)(2,1)S(1)} %bitcast.489), channel_id=1, source_target_pairs={{16,0},{20,4},{24,8},{28,12},{32,16},{36,20},{40,24},{44,28},{48,3... | collective-permute-start | bytes 589832 | tf_op jit(solution)/shard_map/ppermute | solution.py:15
  83.5 23.4 %collective-permute-start.11 = (bf16[256,384]{1,0:T(8,128)(2,1)}, bf16[256,384]{1,0:T(8,128)(2,1)}, u32[]{:S(2)}, u32[]{:S(2)}) collective-permute-start(bf16[256,384]{1,0:T(8,128)(2,1)} %bitcast.9), channel_id=1, source_target_pairs={{16,0},{20,4},{24,8},{28,12},{32,16},{36,20},{40,24},{44,28},{48,3... | collective-permute-start | bytes 589832 | tf_op jit(solution)/shard_map/ppermute | solution.py:15
  89.4 25.7 %collective-permute-start.8 = (bf16[256,384]{1,0:T(8,128)(2,1)S(1)}, bf16[256,384]{1,0:T(8,128)(2,1)S(1)}, u32[]{:S(2)}, u32[]{:S(2)}) collective-permute-start(bf16[256,384]{1,0:T(8,128)(2,1)S(1)} %bitcast.490), channel_id=1, source_target_pairs={{0,16},{4,20},{8,24},{12,28},{16,32},{20,36},{24,40},{28,44},{32,4... | collective-permute-start | bytes 589832 | tf_op jit(solution)/shard_map/ppermute | solution.py:15
  93.8 25.2 %collective-permute-start.9 = (bf16[256,384]{1,0:T(8,128)(2,1)}, bf16[256,384]{1,0:T(8,128)(2,1)S(1)}, u32[]{:S(2)}, u32[]{:S(2)}) collective-permute-start(bf16[256,384]{1,0:T(8,128)(2,1)} %bitcast.9), channel_id=1, source_target_pairs={{0,16},{4,20},{8,24},{12,28},{16,32},{20,36},{24,40},{28,44},{32,4... | collective-permute-start | bytes 589832 | tf_op jit(solution)/shard_map/ppermute | solution.py:15
  98.6 24.8 %collective-permute-start.6 = (bf16[256,384]{1,0:T(8,128)(2,1)S(1)}, bf16[256,384]{1,0:T(8,128)(2,1)}, u32[]{:S(2)}, u32[]{:S(2)}) collective-permute-start(bf16[256,384]{1,0:T(8,128)(2,1)S(1)} %bitcast.491), channel_id=1, source_target_pairs={{8,0},{12,4},{16,8},{20,12},{24,16},{28,20},{32,24},{36,28},{40,32... | collective-permute-start | bytes 589832 | tf_op jit(solution)/shard_map/ppermute | solution.py:15
  103.8 24.0 %collective-permute-start.7 = (bf16[256,384]{1,0:T(8,128)(2,1)}, bf16[256,384]{1,0:T(8,128)(2,1)}, u32[]{:S(2)}, u32[]{:S(2)}) collective-permute-start(bf16[256,384]{1,0:T(8,128)(2,1)} %bitcast.9), channel_id=1, source_target_pairs={{8,0},{12,4},{16,8},{20,12},{24,16},{28,20},{32,24},{36,28},{40,32... | collective-permute-start | bytes 589832 | tf_op jit(solution)/shard_map/ppermute | solution.py:15
  106.9 27.0 %collective-permute-start.4 = (bf16[256,384]{1,0:T(8,128)(2,1)S(1)}, bf16[256,384]{1,0:T(8,128)(2,1)}, u32[]{:S(2)}, u32[]{:S(2)}) collective-permute-start(bf16[256,384]{1,0:T(8,128)(2,1)S(1)} %bitcast.492), channel_id=1, source_target_pairs={{0,8},{4,12},{8,16},{12,20},{16,24},{20,28},{24,32},{28,36},{32,40... | collective-permute-start | bytes 589832 | tf_op jit(solution)/shard_map/ppermute | solution.py:15
  115.0 25.9 %collective-permute-start.5 = (bf16[256,384]{1,0:T(8,128)(2,1)}, bf16[256,384]{1,0:T(8,128)(2,1)}, u32[]{:S(2)}, u32[]{:S(2)}) collective-permute-start(bf16[256,384]{1,0:T(8,128)(2,1)} %bitcast.9), channel_id=1, source_target_pairs={{0,8},{4,12},{8,16},{12,20},{16,24},{20,28},{24,32},{28,36},{32,40... | collective-permute-start | bytes 589832 | tf_op jit(solution)/shard_map/ppermute | solution.py:15
  119.0 38.7 %collective-permute-start.2 = (bf16[256,384]{1,0:T(8,128)(2,1)S(1)}, bf16[256,384]{1,0:T(8,128)(2,1)}, u32[]{:S(2)}, u32[]{:S(2)}) collective-permute-start(bf16[256,384]{1,0:T(8,128)(2,1)S(1)} %bitcast.493), channel_id=1, source_target_pairs={{4,0},{8,4},{12,8},{16,12},{20,16},{24,20},{28,24},{32,28},{36,32}... | collective-permute-start | bytes 589832 | tf_op jit(solution)/shard_map/ppermute | solution.py:15
  123.4 38.5 %collective-permute-start.3 = (bf16[256,384]{1,0:T(8,128)(2,1)}, bf16[256,384]{1,0:T(8,128)(2,1)}, u32[]{:S(2)}, u32[]{:S(2)}) collective-permute-start(bf16[256,384]{1,0:T(8,128)(2,1)} %bitcast.9), channel_id=1, source_target_pairs={{4,0},{8,4},{12,8},{16,12},{20,16},{24,20},{28,24},{32,28},{36,32}... | collective-permute-start | bytes 589832 | tf_op jit(solution)/shard_map/ppermute | solution.py:15
  127.9 43.3 %collective-permute-start = (bf16[256,384]{1,0:T(8,128)(2,1)S(1)}, bf16[256,384]{1,0:T(8,128)(2,1)}, u32[]{:S(2)}, u32[]{:S(2)}) collective-permute-start(bf16[256,384]{1,0:T(8,128)(2,1)S(1)} %bitcast.494), channel_id=1, source_target_pairs={{0,4},{4,8},{8,12},{12,16},{16,20},{20,24},{24,28},{28,32},{32,36}... | collective-permute-start | bytes 589832 | tf_op jit(solution)/shard_map/ppermute | solution.py:15
  133.9 41.5 %collective-permute-start.1 = (bf16[256,384]{1,0:T(8,128)(2,1)}, bf16[256,384]{1,0:T(8,128)(2,1)}, u32[]{:S(2)}, u32[]{:S(2)}) collective-permute-start(bf16[256,384]{1,0:T(8,128)(2,1)} %bitcast.9), channel_id=1, source_target_pairs={{0,4},{4,8},{8,12},{12,16},{16,20},{20,24},{24,28},{28,32},{32,36}... | collective-permute-start | bytes 589832 | tf_op jit(solution)/shard_map/ppermute | solution.py:15
  141.0 48.1 %collective-permute-start.24 = (bf16[256,384]{1,0:T(8,128)(2,1)S(1)}, bf16[256,384]{1,0:T(8,128)(2,1)}, u32[]{:S(2)}, u32[]{:S(2)}) collective-permute-start(bf16[256,384]{1,0:T(8,128)(2,1)S(1)} %bitcast.495), channel_id=1, source_target_pairs={{0,256},{4,260},{8,264},{12,268},{16,272},{20,276},{24,280},{28,28... | collective-permute-start | bytes 589832 | tf_op jit(solution)/shard_map/ppermute | solution.py:15
  157.7 40.7 %collective-permute-start.25 = (bf16[256,384]{1,0:T(8,128)(2,1)}, bf16[256,384]{1,0:T(8,128)(2,1)}, u32[]{:S(2)}, u32[]{:S(2)}) collective-permute-start(bf16[256,384]{1,0:T(8,128)(2,1)} %bitcast.9), channel_id=1, source_target_pairs={{0,256},{4,260},{8,264},{12,268},{16,272},{20,276},{24,280},{28,28... | collective-permute-start | bytes 589832 | tf_op jit(solution)/shard_map/ppermute | solution.py:15
  161.9 43.6 %collective-permute-start.22 = (bf16[256,384]{1,0:T(8,128)(2,1)S(1)}, bf16[256,384]{1,0:T(8,128)(2,1)}, u32[]{:S(2)}, u32[]{:S(2)}) collective-permute-start(bf16[256,384]{1,0:T(8,128)(2,1)S(1)} %bitcast.496), channel_id=1, source_target_pairs={{128,0},{132,4},{136,8},{140,12},{144,16},{148,20},{152,24},{156,2... | collective-permute-start | bytes 589832 | tf_op jit(solution)/shard_map/ppermute | solution.py:15
  171.2 38.2 %collective-permute-start.23 = (bf16[256,384]{1,0:T(8,128)(2,1)}, bf16[256,384]{1,0:T(8,128)(2,1)}, u32[]{:S(2)}, u32[]{:S(2)}) collective-permute-start(bf16[256,384]{1,0:T(8,128)(2,1)} %bitcast.9), channel_id=1, source_target_pairs={{128,0},{132,4},{136,8},{140,12},{144,16},{148,20},{152,24},{156,2... | collective-permute-start | bytes 589832 | tf_op jit(solution)/shard_map/ppermute | solution.py:15
  175.4 39.9 %collective-permute-start.20 = (bf16[256,384]{1,0:T(8,128)(2,1)S(1)}, bf16[256,384]{1,0:T(8,128)(2,1)}, u32[]{:S(2)}, u32[]{:S(2)}) collective-permute-start(bf16[256,384]{1,0:T(8,128)(2,1)S(1)} %bitcast.497), channel_id=1, source_target_pairs={{0,128},{4,132},{8,136},{12,140},{16,144},{20,148},{24,152},{28,15... | collective-permute-start | bytes 589832 | tf_op jit(solution)/shard_map/ppermute | solution.py:15
  189.1 28.5 %collective-permute-start.21 = (bf16[256,384]{1,0:T(8,128)(2,1)}, bf16[256,384]{1,0:T(8,128)(2,1)}, u32[]{:S(2)}, u32[]{:S(2)}) collective-permute-start(bf16[256,384]{1,0:T(8,128)(2,1)} %bitcast.9), channel_id=1, source_target_pairs={{0,128},{4,132},{8,136},{12,140},{16,144},{20,148},{24,152},{28,15... | collective-permute-start | bytes 589832 | tf_op jit(solution)/shard_map/ppermute | solution.py:15
  198.4 50.0 %collective-permute-start.26 = (bf16[256,384]{1,0:T(8,128)(2,1)S(1)}, bf16[256,384]{1,0:T(8,128)(2,1)}, u32[]{:S(2)}, u32[]{:S(2)}) collective-permute-start(bf16[256,384]{1,0:T(8,128)(2,1)S(1)} %bitcast.498), channel_id=1, source_target_pairs={{256,0},{260,4},{264,8},{268,12},{272,16},{276,20},{280,24},{284,2... | collective-permute-start | bytes 589832 | tf_op jit(solution)/shard_map/ppermute | solution.py:15
  205.6 46.3 %collective-permute-start.27 = (bf16[256,384]{1,0:T(8,128)(2,1)}, bf16[256,384]{1,0:T(8,128)(2,1)}, u32[]{:S(2)}, u32[]{:S(2)}) collective-permute-start(bf16[256,384]{1,0:T(8,128)(2,1)} %bitcast.9), channel_id=1, source_target_pairs={{256,0},{260,4},{264,8},{268,12},{272,16},{276,20},{280,24},{284,2... | collective-permute-start | bytes 589832 | tf_op jit(solution)/shard_map/ppermute | solution.py:15
  (48 other events, 283.7 us)
where the time goes:
time: 330 us; the launch traced here: 327 us
  starting transfers between devices  118 us (36%)
  local copies, waits for them, and re-layouts  108 us (33%)
  other arithmetic  40.1 us (12%)
  waiting for transfers between devices  29.7 us (9%)
  blocking collectives  10.9 us (3%)
  matrix products  10.5 us (3%)
  between operations  9.65 us (3%)
    ppermute x28, starting transfers between devices, shifted(): return lax.ppermute(block, axis, route)  106 us
    ppermute x28, waiting for transfers between devices, shifted(): return lax.ppermute(block, axis, route)  26.3 us
    gather x14, local copies, waits for them, and re-layouts, visit(): jnp.take(far_values.reshape(block_count, BLOCK, columns), chosen, axis=0)  25.1 us
    gather x14, local copies, waits for them, and re-layouts, visit(): jnp.take(far_keys.reshape(block_count, BLOCK, columns), chosen, axis=0)  20.8 us
    select_n x14, other arithmetic, visit(): jnp.take(far_values.reshape(block_count, BLOCK, columns), chosen, axis=0)  19.4 us
    unnamed x82, local copies, waits for them, and re-layouts  16.1 us
    select_n x14, local copies, waits for them, and re-layouts, visit(): jnp.take(far_values.reshape(block_count, BLOCK, columns), chosen, axis=0)  15.2 us
    another operation x14, local copies, waits for them, and re-layouts, attend_tile(): value_heads = value_rows.reshape(value_rows.shape[0], head_count, -1)  11.3 us
  transfers between devices with their start and end apart: 31, of which 3 were waited for; matrix products, arithmetic and copies ran while one was open for 28% of the time, Pallas kernels for 0%

commit v1 on v0

v1 whole, which is shorter than its diff:
```python
import functools
import math

import jax
import jax.numpy as jnp
from jax import lax
from jax.experimental import pallas as pl
from jax.experimental.pallas import tpu as pltpu
from jax.sharding import PartitionSpec as P

MESH = pl.DeviceIdType.MESH

NZ, NY, NC, NX = 16, 4, 2, 4
GROUPS = NZ * NY * NC
HEADS = 3
DIM = 128
BLOCK = 128
TOK = 64
ROWS = TOK * NX
HIDE = 1e30
EXPONENT = math.log2(math.e) / math.sqrt(DIM)

OWN = 0
BELOW = 0
ABOVE = 4
M2, P2, M4, P4, SIB, SIB2, VIA_M4, VIA_P4 = 9, 10, 11, 12, 13, 14, 15, 16
SLOTS = 17


def kernel(
    q_hbm, k_hbm, v_hbm, picks_hbm, counts_hbm, out_hbm,
    kv, far, qs, os, acc, top, total, counts, picks,
    in_send, in_recv, in_local, kv_send, kv_recv, long_send, long_recv, short_send, short_recv,
    out_send, out_recv, out_local, small_sem,
):
    me = lax.axis_index("frames")
    mx = lax.axis_index("heads")
    core = lax.rem(me, NC)
    my = lax.rem(me // NC, NY)
    mz = me // (NC * NY)

    def frame(z, y, c):
        return (z * NY + y) * NC + c

    up = (frame(lax.rem(mz + 1, NZ), my, core), mx)
    down = (frame(lax.rem(mz + NZ - 1, NZ), my, core), mx)
    right = (frame(mz, lax.rem(my + 1, NY), core), mx)
    left = (frame(mz, lax.rem(my + NY - 1, NY), core), mx)
    sibling = (frame(mz, my, 1 - core), mx)
    others = [(me, lax.rem(mx + d, NX)) for d in (1, 2, 3)]

    table = [
        pltpu.make_async_copy(counts_hbm.at[pl.ds(me, 1)], counts, small_sem.at[0]),
        pltpu.make_async_copy(picks_hbm.at[me], picks, small_sem.at[1]),
    ]
    for copy in table:
        copy.start()

    barrier = pltpu.get_barrier_semaphore()
    partners = [up, down, right, left, sibling] + others
    for partner in partners:
        pl.semaphore_signal(barrier, inc=1, device_id=partner, device_id_type=MESH)
    pl.semaphore_wait(barrier, len(partners))

    def landing(t, h, x):
        rows = pl.ds(pl.multiple_of(x * TOK, TOK), TOK)
        if t == 2:
            return qs.at[h, rows, :]
        return kv.at[OWN, h, t, rows, :]

    def piece(t, h, x):
        source = (k_hbm, v_hbm, q_hbm)[t]
        return source.at[:, pl.ds(pl.multiple_of((x * HEADS + h) * DIM, DIM), DIM)]

    def exchange(t, h, d):
        target = lax.rem(mx + d, NX)
        return pltpu.make_async_remote_copy(
            src_ref=piece(t, h, target),
            dst_ref=landing(t, h, mx),
            send_sem=in_send.at[t, h, d - 1],
            recv_sem=in_recv.at[t, h, d - 1],
            device_id=(me, target),
            device_id_type=MESH,
        )

    def kept(t, h):
        return pltpu.make_async_copy(piece(t, h, mx), landing(t, h, mx), in_local.at[t, h])

    def arrived(t, h):
        kept(t, h).wait()
        for d in (1, 2, 3):
            source = lax.rem(mx + NX - d, NX)
            there = landing(t, h, source)
            pltpu.make_async_copy(there, there, in_recv.at[t, h, d - 1]).wait()

    for h in range(HEADS):
        for t in (0, 1):
            for d in (2, 1, 3):
                exchange(t, h, d).start()
            kept(t, h).start()
    for h in range(HEADS):
        for d in (2, 1, 3):
            exchange(2, h, d).start()
        kept(2, h).start()

    def pass_on(source, slot, h, target):
        return pltpu.make_async_remote_copy(
            src_ref=kv.at[source, h],
            dst_ref=kv.at[slot, h],
            send_sem=kv_send.at[slot - M2, h],
            recv_sem=kv_recv.at[slot - M2, h],
            device_id=target,
            device_id_type=MESH,
        )

    def await_slot(slot, h):
        there = kv.at[slot, h]
        pltpu.make_async_copy(there, there, kv_recv.at[slot - M2, h]).wait()

    ways = (up, down)
    depth = (mz, NZ - 1 - mz)

    def held(way, k, h, t):
        if k == 0:
            return kv.at[OWN, h, t]
        if k <= 4:
            return kv.at[(BELOW, ABOVE)[way] + k, h, t]
        return far.at[k - 5, way, h]

    def pass_along(way, k, h, t, send, recv):
        return pltpu.make_async_remote_copy(
            src_ref=held(way, k - 1, h, t),
            dst_ref=held(way, k, h, t),
            send_sem=send.at[way, k - 1, h],
            recv_sem=recv.at[way, k - 1, h],
            device_id=ways[way],
            device_id_type=MESH,
        )

    def pass_long(way, k, h):
        return pass_along(way, k, h, way, long_send, long_recv)

    def pass_short(way, k, h):
        return pass_along(way, k, h, 1 - way, short_send, short_recv)

    def takes(way, k):
        d = depth[way]
        return ((d >= 3) & (d <= NZ - 2)) if k == 3 else d >= k

    def gives(way, k):
        d = depth[way]
        return ((d >= 2) & (d <= NZ - 3)) if k == 3 else (d >= k - 1) & (d <= NZ - 2)

    def long_hop(k, h):
        for way in (0, 1):
            there = held(way, k, h, way)
            pltpu.make_async_copy(there, there, long_recv.at[way, k - 1, h]).wait()
            if k < 8:
                pass_long(way, k + 1, h).start()

    def short_hop(k, h):
        for way in (0, 1):
            @pl.when(takes(way, k))
            def _():
                there = held(way, k, h, 1 - way)
                pltpu.make_async_copy(there, there, short_recv.at[way, k - 1, h]).wait()

            if k < 4:
                @pl.when(gives(way, k + 1))
                def _():
                    pass_short(way, k + 1, h).start()

    for way in (0, 1):
        for k in (1, 2, 4):
            @pl.when(jnp.logical_not(takes(way, k)))
            def _():
                slot = (BELOW, ABOVE)[way] + k
                for h in range(HEADS):
                    kv[slot, h, 1 - way] = jnp.zeros((ROWS, DIM), jnp.bfloat16)

    for h in range(HEADS):
        arrived(0, h)
        arrived(1, h)
        for way in (0, 1):
            pass_long(way, 1, h).start()
    for way in (0, 1):
        @pl.when(gives(way, 1))
        def _():
            for h in range(HEADS):
                pass_short(way, 1, h).start()
    for copy in table:
        copy.wait()

    def bias_of(group):
        inside = (group >= 0) & (group < GROUPS)
        row = jnp.clip(group, 0, GROUPS - 1)
        count = jnp.where(inside, counts[0, row], 0)
        first, second = picks[0, row], picks[1, row]
        return [
            jnp.where(((count > 0) & (first == j)) | ((count > 1) & (second == j)), 0.0, -HIDE)
            for j in (0, 1)
        ]

    def attend(h, parts, fresh=False):
        query = qs[h]
        raw, highs = [], []
        for keys, values, biases in parts:
            s = lax.dot_general(
                keys, query, (((1,), (1,)), ((), ())), preferred_element_type=jnp.float32
            )
            for j in (0, 1):
                block = s[j * BLOCK:(j + 1) * BLOCK]
                high = jnp.max(block, axis=0, keepdims=True)
                raw.append(block)
                highs.append(high if biases is None else high + biases[j])
        newest = functools.reduce(jnp.maximum, highs)
        if not fresh:
            newest = jnp.maximum(newest, top[h])
        row_sum, mixed = None, None
        for i, (keys, values, biases) in enumerate(parts):
            weights = []
            for j in (0, 1):
                level = newest if biases is None else newest - biases[j]
                w = jnp.exp2((raw[2 * i + j] - level) * EXPONENT)
                weights.append(w.astype(jnp.bfloat16))
                folded = jnp.sum(w.reshape(BLOCK // 8, 8, ROWS), axis=0)
                row_sum = folded if row_sum is None else row_sum + folded
            weight = jnp.concatenate(weights, axis=0)
            product = lax.dot_general(
                values, weight, (((0,), (0,)), ((), ())), preferred_element_type=jnp.float32
            )
            mixed = product if mixed is None else mixed + product
        if not fresh:
            rescale = jnp.exp2((top[h] - newest) * EXPONENT)
            row_sum = row_sum + total[h] * rescale
            mixed = mixed + acc[h] * rescale
        top[h] = newest
        total[h] = row_sum
        acc[h] = mixed

    def part(slot, h, group):
        return kv[slot, h, 0], kv[slot, h, 1], bias_of(group)

    def over_heads(body):
        def step(h, carry):
            body(h)
            return carry

        lax.fori_loop(0, HEADS, step, 0)

    ZSTEP = NY * NC

    def near(k, h):
        attend(h, [part(BELOW + k, h, me - k * ZSTEP), part(ABOVE + k, h, me + k * ZSTEP)])

    def long_1(h):
        long_hop(1, h)
        pass_on(OWN, SIB, h, sibling).start()
        arrived(2, h)
        attend(h, [(kv[OWN, h, 0], kv[OWN, h, 1], None)], fresh=True)

    def short_1(h):
        short_hop(1, h)
        pass_on(jnp.where(my == NY - 1, BELOW + 1, OWN), M2, h, right).start()
        near(1, h)

    def long_2(h):
        long_hop(2, h)
        pass_on(jnp.where(my == 0, ABOVE + 1, OWN), P2, h, left).start()

    def short_2(h):
        short_hop(2, h)

        @pl.when(my == 2)
        def _():
            pass_on(BELOW + 1, VIA_M4, h, right).start()

        @pl.when(my == 1)
        def _():
            pass_on(ABOVE + 1, VIA_P4, h, left).start()

        near(2, h)

    def long_4(h):
        long_hop(4, h)
        await_slot(M2, h)
        await_slot(P2, h)
        pass_on(jnp.where(core == 1, M2, P2), SIB2, h, sibling).start()

        @pl.when(my == NY - 1)
        def _():
            await_slot(VIA_M4, h)

        pass_on(jnp.where(my == NY - 1, VIA_M4, M2), M4, h, right).start()
        attend(h, [part(M2, h, me - 2), part(P2, h, me + 2)])

    def long_5(h):
        long_hop(5, h)

        @pl.when(my == 0)
        def _():
            await_slot(VIA_P4, h)

        pass_on(jnp.where(my == 0, VIA_P4, P2), P4, h, left).start()

    def long_6(h):
        long_hop(6, h)
        await_slot(SIB, h)
        await_slot(SIB2, h)
        attend(h, [part(SIB, h, me + 1 - 2 * core), part(SIB2, h, me - 1 + 2 * core)])

    def long_7(h):
        long_hop(7, h)
        await_slot(M4, h)
        await_slot(P4, h)
        attend(h, [part(M4, h, me - 4), part(P4, h, me + 4)])

    def short_4(h):
        short_hop(4, h)
        near(4, h)

    over_heads(long_1)
    over_heads(short_1)
    over_heads(long_2)
    over_heads(short_2)
    over_heads(functools.partial(long_hop, 3))
    over_heads(long_4)
    over_heads(long_5)
    over_heads(long_6)
    over_heads(functools.partial(short_hop, 3))
    over_heads(long_7)
    over_heads(short_4)

    def out_columns(x, h):
        return out_hbm.at[:, pl.ds(pl.multiple_of((x * HEADS + h) * DIM, DIM), DIM)]

    def out_rows(x, h):
        return os.at[h, pl.ds(pl.multiple_of(x * TOK, TOK), TOK), :]

    def give_back(h, d):
        target = lax.rem(mx + d, NX)
        return pltpu.make_async_remote_copy(
            src_ref=out_rows(target, h),
            dst_ref=out_columns(mx, h),
            send_sem=out_send.at[h, d - 1],
            recv_sem=out_recv.at[h, d - 1],
            device_id=(me, target),
            device_id_type=MESH,
        )

    def keep_back(h):
        return pltpu.make_async_copy(out_rows(mx, h), out_columns(mx, h), out_local.at[h])

    def eighth(h):
        long_hop(8, h)
        opposite = lax.rem(me + 8 * ZSTEP, GROUPS)
        attend(h, [(far[3, 0, h], far[3, 1, h], bias_of(opposite))])
        row_total = jnp.sum(total[h], axis=0, keepdims=True)
        os[h] = jnp.transpose(acc[h] / row_total).astype(jnp.bfloat16)
        for d in (2, 1, 3):
            give_back(h, d).start()
        keep_back(h).start()

    over_heads(eighth)

    def finish(h):
        for t in (0, 1, 2):
            for d in (1, 2, 3):
                exchange(t, h, d).wait_send()
        for slot in range(M2, VIA_M4):
            pass_on(OWN, slot, h, sibling).wait_send()
        for slot, place in ((VIA_M4, 2), (VIA_P4, 1)):
            @pl.when(my == place)
            def _():
                pass_on(OWN, slot, h, sibling).wait_send()
        for way in (0, 1):
            for k in range(1, 9):
                pass_long(way, k, h).wait_send()
            for k in range(1, 5):
                @pl.when(gives(way, k))
                def _():
                    pass_short(way, k, h).wait_send()
        for d in (1, 2, 3):
            give_back(h, d).wait_send()
        keep_back(h).wait()
        for d in (1, 2, 3):
            there = out_columns(lax.rem(mx + NX - d, NX), h)
            pltpu.make_async_copy(there, there, out_recv.at[h, d - 1]).wait()

    over_heads(finish)


def local(queries, keys, values, block_picks, block_counts):
    picks = jnp.transpose(block_picks, (0, 2, 1))
    dma = pltpu.SemaphoreType.DMA
    return pl.pallas_call(
        kernel,
        out_shape=jax.ShapeDtypeStruct(queries.shape, queries.dtype),
        in_specs=[pl.BlockSpec(memory_space=pltpu.HBM)] * 5,
        out_specs=pl.BlockSpec(memory_space=pl.ANY),
        scratch_shapes=[
            pltpu.VMEM((SLOTS, HEADS, 2, ROWS, DIM), jnp.bfloat16),
            pltpu.VMEM((4, 2, HEADS, ROWS, DIM), jnp.bfloat16),
            pltpu.VMEM((HEADS, ROWS, DIM), jnp.bfloat16),
            pltpu.VMEM((HEADS, ROWS, DIM), jnp.bfloat16),
            pltpu.VMEM((HEADS, DIM, ROWS), jnp.float32),
            pltpu.VMEM((HEADS, 1, ROWS), jnp.float32),
            pltpu.VMEM((HEADS, 8, ROWS), jnp.float32),
            pltpu.SMEM((1, GROUPS), jnp.int32),
            pltpu.SMEM((2, GROUPS), jnp.int32),
            dma((3, HEADS, 3)), dma((3, HEADS, 3)), dma((3, HEADS)),
            dma((SLOTS - M2, HEADS)), dma((SLOTS - M2, HEADS)),
            dma((2, 8, HEADS)), dma((2, 8, HEADS)), dma((2, 4, HEADS)), dma((2, 4, HEADS)),
            dma((HEADS, 3)), dma((HEADS, 3)), dma((HEADS,)), dma((2,)),
        ],
        compiler_params=pltpu.CompilerParams(
            collective_id=0, has_side_effects=True, vmem_limit_bytes=60 * 1024 * 1024
        ),
        name="radial_attention",
    )(queries, keys, values, picks, block_counts)


def solution(mesh):
    placed = P(("frames", "heads"), None)
    return jax.shard_map(
        local,
        mesh=mesh,
        in_specs=(placed, placed, placed, P(), P()),
        out_specs=placed,
        check_vma=False,
    )
```

time: 330 us -> 73.7 us (0.22)
  the two profiles are of different devices: /device:TPU:152 before, /device:TPU:2 now
where the time goes in v1:
time: 73.7 us; the launch traced here: 73.5 us
  Pallas kernels  71.9 us (98%)
  local copies, waits for them, and re-layouts  1.62 us (2%)
    pallas_call x1, Pallas kernels, local(): pl.pallas_call(kernel, out_shape=jax.ShapeDtypeStruct(queries.shape, quer...  71.9 us
    unnamed x1, local copies, waits for them, and re-layouts  1.62 us

profile of v1, /device:TPU:2, one launch (start us, length us, event | category | flops | bytes accessed | tf_op | source)
XLA Modules:
  0.0 73.5 jit_solution(4326837910891161900)
XLA Ops:
  0.0 71.9 %radial_attention.1 = bf16[64,1536]{1,0:T(8,128)(2,1)} custom-call(bf16[64,1536]{1,0:T(8,128)(2,1)} %q_hbm.1, bf16[64,1536]{1,0:T(8,128)(2,1)} %k_hbm.1, bf16[64,1536]{1,0:T(8,128)(2,1)} %v_hbm.1, s32[128,2,128]{2,1,0:T(2,128)} %bitcast.1, s32[128,128]{1,0:T(8,128)} %counts_hbm.1), custom_call_target="tpu_custom_call" | custom-call | tf_op jit(solution)/shard_map/radial_attention/pallas_call | solution.py:396
  71.9 1.6 %copy.7 = bf16[64,1536]{1,0:T(8,128)(2,1)} copy(bf16[64,1536]{1,0:T(8,128)(2,1)} %radial_attention.1) | data formatting | bytes 393216

commit v2 on v1

--- a/solution.py
+++ b/solution.py
@@ -22,14 +22,26 @@
 
 OWN = 0
 BELOW = 0
-ABOVE = 4
-M2, P2, M4, P4, SIB, SIB2, VIA_M4, VIA_P4 = 9, 10, 11, 12, 13, 14, 15, 16
-SLOTS = 17
+ABOVE = 8
+M2, P2, M4, P4, SIB, SIB2, VIA_M4, VIA_P4 = 17, 18, 19, 20, 21, 22, 23, 24
+SLOTS = 25
+
+STAGES = (
+    ("long", 1), ("long", 2), ("long", 3), ("short", 1), ("long", 4), ("long", 5),
+    ("short", 2), ("long", 6), ("short", 3), ("long", 7), ("short", 4), ("long", 8),
+)
+
+
+def pick(index, values):
+    found = values[-1]
+    for i, value in enumerate(values[:-1]):
+        found = jnp.where(index == i, value, found)
+    return found
 
 
 def kernel(
     q_hbm, k_hbm, v_hbm, picks_hbm, counts_hbm, out_hbm,
-    kv, far, qs, os, acc, top, total, counts, picks,
+    kv, qs, os, acc, top, total, counts, picks,
     in_send, in_recv, in_local, kv_send, kv_recv, long_send, long_recv, short_send, short_recv,
     out_send, out_recv, out_local, small_sem,
 ):
@@ -93,15 +105,21 @@
             there = landing(t, h, source)
             pltpu.make_async_copy(there, there, in_recv.at[t, h, d - 1]).wait()
 
-    for h in range(HEADS):
-        for t in (0, 1):
+    def over_heads(body):
+        def step(h, carry):
+            body(h)
+            return carry
+
+        lax.fori_loop(0, HEADS, step, 0)
+
+    def send_pieces(tensors, h):
+        for t in tensors:
             for d in (2, 1, 3):
                 exchange(t, h, d).start()
             kept(t, h).start()
-    for h in range(HEADS):
-        for d in (2, 1, 3):
-            exchange(2, h, d).start()
-        kept(2, h).start()
+
+    over_heads(functools.partial(send_pieces, (0, 1)))
+    over_heads(functools.partial(send_pieces, (2,)))
 
     def pass_on(source, slot, h, target):
         return pltpu.make_async_remote_copy(
@@ -121,11 +139,7 @@
     depth = (mz, NZ - 1 - mz)
 
     def held(way, k, h, t):
-        if k == 0:
-            return kv.at[OWN, h, t]
-        if k <= 4:
-            return kv.at[(BELOW, ABOVE)[way] + k, h, t]
-        return far.at[k - 5, way, h]
+        return kv.at[jnp.where(k == 0, OWN, (BELOW, ABOVE)[way] + k), h, t]
 
     def pass_along(way, k, h, t, send, recv):
         return pltpu.make_async_remote_copy(
@@ -145,17 +159,19 @@
 
     def takes(way, k):
         d = depth[way]
-        return ((d >= 3) & (d <= NZ - 2)) if k == 3 else d >= k
+        return (d >= k) & ((k != 3) | (d <= NZ - 2))
 
     def gives(way, k):
         d = depth[way]
-        return ((d >= 2) & (d <= NZ - 3)) if k == 3 else (d >= k - 1) & (d <= NZ - 2)
+        return (d >= k - 1) & (d <= jnp.where(k == 3, NZ - 3, NZ - 2))
 
     def long_hop(k, h):
         for way in (0, 1):
             there = held(way, k, h, way)
             pltpu.make_async_copy(there, there, long_recv.at[way, k - 1, h]).wait()
-            if k < 8:
+
+            @pl.when(k < 8)
+            def _():
                 pass_long(way, k + 1, h).start()
 
     def short_hop(k, h):
@@ -165,10 +181,9 @@
                 there = held(way, k, h, 1 - way)
                 pltpu.make_async_copy(there, there, short_recv.at[way, k - 1, h]).wait()
 
-            if k < 4:
-                @pl.when(gives(way, k + 1))
-                def _():
-                    pass_short(way, k + 1, h).start()
+            @pl.when((k < 4) & gives(way, k + 1))
+            def _():
+                pass_short(way, k + 1, h).start()
 
     for way in (0, 1):
         for k in (1, 2, 4):
@@ -178,16 +193,21 @@
                 for h in range(HEADS):
                     kv[slot, h, 1 - way] = jnp.zeros((ROWS, DIM), jnp.bfloat16)
 
-    for h in range(HEADS):
+    def start_long(h):
         arrived(0, h)
         arrived(1, h)
         for way in (0, 1):
             pass_long(way, 1, h).start()
-    for way in (0, 1):
-        @pl.when(gives(way, 1))
-        def _():
-            for h in range(HEADS):
+        pass_on(OWN, SIB, h, sibling).start()
+
+    def start_short(h):
+        for way in (0, 1):
+            @pl.when(gives(way, 1))
+            def _():
                 pass_short(way, 1, h).start()
+
+    over_heads(start_long)
+    over_heads(start_short)
     for copy in table:
         copy.wait()
 
@@ -197,139 +217,144 @@
         count = jnp.where(inside, counts[0, row], 0)
         first, second = picks[0, row], picks[1, row]
         return [
-            jnp.where(((count > 0) & (first == j)) | ((count > 1) & (second == j)), 0.0, -HIDE)
+            jnp.where(
+                (group == me) | ((count > 0) & (first == j)) | ((count > 1) & (second == j)), 0.0, -HIDE
+            )
             for j in (0, 1)
         ]
 
-    def attend(h, parts, fresh=False):
+    def attend(h, parts):
         query = qs[h]
-        raw, highs = [], []
-        for keys, values, biases in parts:
+        raw, biases, highs = [], [], []
+        for key_slot, _, group in parts:
             s = lax.dot_general(
-                keys, query, (((1,), (1,)), ((), ())), preferred_element_type=jnp.float32
+                kv[key_slot, h, 0], query, (((1,), (1,)), ((), ())), preferred_element_type=jnp.float32
             )
-            for j in (0, 1):
+            for j, bias in enumerate(bias_of(group)):
                 block = s[j * BLOCK:(j + 1) * BLOCK]
-                high = jnp.max(block, axis=0, keepdims=True)
                 raw.append(block)
-                highs.append(high if biases is None else high + biases[j])
-        newest = functools.reduce(jnp.maximum, highs)
-        if not fresh:
-            newest = jnp.maximum(newest, top[h])
-        row_sum, mixed = None, None
-        for i, (keys, values, biases) in enumerate(parts):
+                biases.append(bias)
+                highs.append(jnp.max(block, axis=0, keepdims=True) + bias)
+        newest = functools.reduce(jnp.maximum, highs + [top[h]])
+        rescale = jnp.exp2((top[h] - newest) * EXPONENT)
+        row_sum = total[h] * rescale
+        mixed = acc[h] * rescale
+        for i, (_, value_slot, _) in enumerate(parts):
             weights = []
-            for j in (0, 1):
-                level = newest if biases is None else newest - biases[j]
-                w = jnp.exp2((raw[2 * i + j] - level) * EXPONENT)
+            for j in (2 * i, 2 * i + 1):
+                w = jnp.exp2((raw[j] - (newest - biases[j])) * EXPONENT)
                 weights.append(w.astype(jnp.bfloat16))
-                folded = jnp.sum(w.reshape(BLOCK // 8, 8, ROWS), axis=0)
-                row_sum = folded if row_sum is None else row_sum + folded
-            weight = jnp.concatenate(weights, axis=0)
-            product = lax.dot_general(
-                values, weight, (((0,), (0,)), ((), ())), preferred_element_type=jnp.float32
+                row_sum = row_sum + jnp.sum(w.reshape(BLOCK // 8, 8, ROWS), axis=0)
+            mixed = mixed + lax.dot_general(
+                kv[value_slot, h, 1], jnp.concatenate(weights, axis=0),
+                (((0,), (0,)), ((), ())), preferred_element_type=jnp.float32,
             )
-            mixed = product if mixed is None else mixed + product
-        if not fresh:
-            rescale = jnp.exp2((top[h] - newest) * EXPONENT)
-            row_sum = row_sum + total[h] * rescale
-            mixed = mixed + acc[h] * rescale
         top[h] = newest
         total[h] = row_sum
         acc[h] = mixed
 
-    def part(slot, h, group):
-        return kv[slot, h, 0], kv[slot, h, 1], bias_of(group)
-
-    def over_heads(body):
-        def step(h, carry):
-            body(h)
-            return carry
-
-        lax.fori_loop(0, HEADS, step, 0)
-
-    ZSTEP = NY * NC
-
-    def near(k, h):
-        attend(h, [part(BELOW + k, h, me - k * ZSTEP), part(ABOVE + k, h, me + k * ZSTEP)])
-
-    def long_1(h):
-        long_hop(1, h)
-        pass_on(OWN, SIB, h, sibling).start()
-        arrived(2, h)
-        attend(h, [(kv[OWN, h, 0], kv[OWN, h, 1], None)], fresh=True)
-
-    def short_1(h):
-        short_hop(1, h)
-        pass_on(jnp.where(my == NY - 1, BELOW + 1, OWN), M2, h, right).start()
-        near(1, h)
-
-    def long_2(h):
-        long_hop(2, h)
-        pass_on(jnp.where(my == 0, ABOVE + 1, OWN), P2, h, left).start()
-
-    def short_2(h):
-        short_hop(2, h)
-
-        @pl.when(my == 2)
+    top[...] = jnp.full(top.shape, -HIDE, jnp.float32)
+    total[...] = jnp.zeros(total.shape, jnp.float32)
+    acc[...] = jnp.zeros(acc.shape, jnp.float32)
+
+    zstep = NY * NC
+    own_pair = ((OWN, OWN, me), (SIB, SIB, me + 1 - 2 * core))
+    far = lax.rem(me + 8 * zstep, GROUPS)
+    last_pair = ((SIB2, SIB2, me - 1 + 2 * core), (BELOW + 8, ABOVE + 8, far))
+
+    def near(k):
+        return (
+            (BELOW + k, BELOW + k, me - k * zstep),
+            (ABOVE + k, ABOVE + k, me + k * zstep),
+        )
+
+    two_pair = ((M2, M2, me - 2), (P2, P2, me + 2))
+    four_pair = ((M4, M4, me - 4), (P4, P4, me + 4))
+    pairs = {0: own_pair, 4: near(1), 6: two_pair, 7: near(2), 9: four_pair, 10: near(4), 11: last_pair}
+
+    def chosen(stage, side):
+        table = [pairs.get(i, own_pair)[side] for i in range(len(STAGES))]
+        return tuple(pick(stage, [entry[field] for entry in table]) for field in range(3))
+
+    def extras(stage, h):
+        @pl.when(stage == 0)
+        def _():
+            arrived(2, h)
+            await_slot(SIB, h)
+
+        @pl.when(((stage == 0) & (my < NY - 1)) | ((stage == 3) & (my == NY - 1)))
+        def _():
+            pass_on(jnp.where(my == NY - 1, BELOW + 1, OWN), M2, h, right).start()
+
+        @pl.when(((stage == 1) & (my > 0)) | ((stage == 3) & (my == 0)))
+        def _():
+            pass_on(jnp.where(my == 0, ABOVE + 1, OWN), P2, h, left).start()
+
+        @pl.when((stage == 3) & (my == 2))
         def _():
             pass_on(BELOW + 1, VIA_M4, h, right).start()
 
-        @pl.when(my == 1)
+        @pl.when((stage == 3) & (my == 1))
         def _():
             pass_on(ABOVE + 1, VIA_P4, h, left).start()
 
-        near(2, h)
-
-    def long_4(h):
-        long_hop(4, h)
-        await_slot(M2, h)
-        await_slot(P2, h)
-        pass_on(jnp.where(core == 1, M2, P2), SIB2, h, sibling).start()
-
-        @pl.when(my == NY - 1)
-        def _():
-            await_slot(VIA_M4, h)
-
-        pass_on(jnp.where(my == NY - 1, VIA_M4, M2), M4, h, right).start()
-        attend(h, [part(M2, h, me - 2), part(P2, h, me + 2)])
-
-    def long_5(h):
-        long_hop(5, h)
-
-        @pl.when(my == 0)
-        def _():
-            await_slot(VIA_P4, h)
-
-        pass_on(jnp.where(my == 0, VIA_P4, P2), P4, h, left).start()
-
-    def long_6(h):
-        long_hop(6, h)
-        await_slot(SIB, h)
-        await_slot(SIB2, h)
-        attend(h, [part(SIB, h, me + 1 - 2 * core), part(SIB2, h, me - 1 + 2 * core)])
-
-    def long_7(h):
-        long_hop(7, h)
-        await_slot(M4, h)
-        await_slot(P4, h)
-        attend(h, [part(M4, h, me - 4), part(P4, h, me + 4)])
-
-    def short_4(h):
-        short_hop(4, h)
-        near(4, h)
-
-    over_heads(long_1)
-    over_heads(short_1)
-    over_heads(long_2)
-    over_heads(short_2)
-    over_heads(functools.partial(long_hop, 3))
-    over_heads(long_4)
-    over_heads(long_5)
-    over_heads(long_6)
-    over_heads(functools.partial(short_hop, 3))
-    over_heads(long_7)
-    over_heads(short_4)
+        @pl.when(stage == 6)
+        def _():
+            await_slot(M2, h)
+            await_slot(P2, h)
+            pass_on(jnp.where(core == 1, M2, P2), SIB2, h, sibling).start()
+
+        @pl.when(stage == 7)
+        def _():
+            @pl.when(my == NY - 1)
+            def _():
+                await_slot(VIA_M4, h)
+
+            @pl.when(my == 0)
+            def _():
+                await_slot(VIA_P4, h)
+
+            pass_on(jnp.where(my == NY - 1, VIA_M4, M2), M4, h, right).start()
+            pass_on(jnp.where(my == 0, VIA_P4, P2), P4, h, left).start()
+
+        @pl.when(stage == 9)
+        def _():
+            await_slot(M4, h)
+            await_slot(P4, h)
+
+        @pl.when(stage == 11)
+        def _():
+            await_slot(SIB2, h)
+
+    def one_stage(stage, carry):
+        hop = pick(stage, [k for _, k in STAGES])
+        is_long = functools.reduce(
+            jnp.logical_and, [stage != i for i, (kind, _) in enumerate(STAGES) if kind == "short"]
+        )
+        attends = functools.reduce(jnp.logical_or, [stage == i for i in pairs])
+        first, second = chosen(stage, 0), chosen(stage, 1)
+
+        def one_head(h):
+            @pl.when(is_long)
+            def _():
+                long_hop(hop, h)
+
+            @pl.when(jnp.logical_not(is_long))
+            def _():
+                short_hop(hop, h)
+
+            extras(stage, h)
+
+            @pl.when(attends)
+            def _():
+                attend(h, [first, second])
+
+            @pl.when(stage == len(STAGES) - 1)
+            def _():
+                finish_head(h)
+
+        over_heads(one_head)
+        return carry
 
     def out_columns(x, h):
         return out_hbm.at[:, pl.ds(pl.multiple_of((x * HEADS + h) * DIM, DIM), DIM)]
@@ -351,17 +376,14 @@
     def keep_back(h):
         return pltpu.make_async_copy(out_rows(mx, h), out_columns(mx, h), out_local.at[h])
 
-    def eighth(h):
-        long_hop(8, h)
-        opposite = lax.rem(me + 8 * ZSTEP, GROUPS)
-        attend(h, [(far[3, 0, h], far[3, 1, h], bias_of(opposite))])
+    def finish_head(h):
         row_total = jnp.sum(total[h], axis=0, keepdims=True)
         os[h] = jnp.transpose(acc[h] / row_total).astype(jnp.bfloat16)
         for d in (2, 1, 3):
             give_back(h, d).start()
         keep_back(h).start()
 
-    over_heads(eighth)
+    lax.fori_loop(0, len(STAGES), one_stage, 0)
 
     def finish(h):
         for t in (0, 1, 2):
@@ -400,7 +422,6 @@
         out_specs=pl.BlockSpec(memory_space=pl.ANY),
         scratch_shapes=[
             pltpu.VMEM((SLOTS, HEADS, 2, ROWS, DIM), jnp.bfloat16),
-            pltpu.VMEM((4, 2, HEADS, ROWS, DIM), jnp.bfloat16),
             pltpu.VMEM((HEADS, ROWS, DIM), jnp.bfloat16),
             pltpu.VMEM((HEADS, ROWS, DIM), jnp.bfloat16),
             pltpu.VMEM((HEADS, DIM, ROWS), jnp.float32),
@@ -414,10 +435,10 @@
             dma((HEADS, 3)), dma((HEADS, 3)), dma((HEADS,)), dma((2,)),
         ],
         compiler_params=pltpu.CompilerParams(
-            collective_id=0, has_side_effects=True, vmem_limit_bytes=60 * 1024 * 1024
+            collective_id=0, has_side_effects=True, vmem_limit_bytes=32 * 1024 * 1024
         ),
         name="radial_attention",
-    )(queries, keys, values, picks, block_counts)
+    )(*(pltpu.with_memory_space_constraint(x, pltpu.HBM) for x in (queries, keys, values, picks, block_counts)))
 
 
 def solution(mesh):

time: 73.7 us -> 71.9 us (0.976)
  the two profiles are of different devices: /device:TPU:2 before, /device:TPU:40 now
where the time goes in v2:
time: 71.9 us; the launch traced here: 71.8 us
  Pallas kernels  71.1 us (99%)
    pallas_call x1, Pallas kernels, local(): pl.pallas_call(kernel, out_shape=jax.ShapeDtypeStruct(queries.shape, quer...  71.1 us

profile of v2, /device:TPU:40, one launch (start us, length us, event | category | flops | bytes accessed | tf_op | source)
XLA Modules:
  0.0 71.8 jit_solution(9454094904107004599)
XLA Ops:
  0.0 71.1 %radial_attention.1 = bf16[64,1536]{1,0:T(8,128)(2,1)S(1)} custom-call(bf16[64,1536]{1,0:T(8,128)(2,1)} %q_hbm.1, bf16[64,1536]{1,0:T(8,128)(2,1)} %k_hbm.1, bf16[64,1536]{1,0:T(8,128)(2,1)} %v_hbm.1, s32[128,2,128]{2,1,0:T(2,128)} %bitcast.1, s32[128,128]{1,0:T(8,128)} %counts_hbm.1), custom_call_target="tpu_custom_call" | custom-call | tf_op jit(solution)/shard_map/radial_attention/pallas_call | solution.py:418
  71.1 0.7 copy.7

commit v3 on v2

--- a/solution.py
+++ b/solution.py
@@ -41,7 +41,7 @@
 
 def kernel(
     q_hbm, k_hbm, v_hbm, picks_hbm, counts_hbm, out_hbm,
-    kv, qs, os, acc, top, total, counts, picks,
+    kv, staged, qs, os, acc, top, total, counts, picks,
     in_send, in_recv, in_local, kv_send, kv_recv, long_send, long_recv, short_send, short_recv,
     out_send, out_recv, out_local, small_sem,
 ):
@@ -65,7 +65,11 @@
         pltpu.make_async_copy(counts_hbm.at[pl.ds(me, 1)], counts, small_sem.at[0]),
         pltpu.make_async_copy(picks_hbm.at[me], picks, small_sem.at[1]),
     ]
-    for copy in table:
+    staging = [
+        pltpu.make_async_copy(source, staged.at[t], small_sem.at[2 + t])
+        for t, source in enumerate((k_hbm, v_hbm, q_hbm))
+    ]
+    for copy in staging + table:
         copy.start()
 
     barrier = pltpu.get_barrier_semaphore()
@@ -81,8 +85,7 @@
         return kv.at[OWN, h, t, rows, :]
 
     def piece(t, h, x):
-        source = (k_hbm, v_hbm, q_hbm)[t]
-        return source.at[:, pl.ds(pl.multiple_of((x * HEADS + h) * DIM, DIM), DIM)]
+        return staged.at[t, :, pl.ds(pl.multiple_of((x * HEADS + h) * DIM, DIM), DIM)]
 
     def exchange(t, h, d):
         target = lax.rem(mx + d, NX)
@@ -118,8 +121,10 @@
                 exchange(t, h, d).start()
             kept(t, h).start()
 
-    over_heads(functools.partial(send_pieces, (0, 1)))
-    over_heads(functools.partial(send_pieces, (2,)))
+    staging[0].wait()
+    staging[1].wait()
+    send_pieces((0, 1), 0)
+    send_pieces((0, 1), 1)
 
     def pass_on(source, slot, h, target):
         return pltpu.make_async_remote_copy(
@@ -194,11 +199,9 @@
                     kv[slot, h, 1 - way] = jnp.zeros((ROWS, DIM), jnp.bfloat16)
 
     def start_long(h):
-        arrived(0, h)
-        arrived(1, h)
         for way in (0, 1):
+            arrived(way, h)
             pass_long(way, 1, h).start()
-        pass_on(OWN, SIB, h, sibling).start()
 
     def start_short(h):
         for way in (0, 1):
@@ -206,8 +209,14 @@
             def _():
                 pass_short(way, 1, h).start()
 
-    over_heads(start_long)
+    start_long(0)
+    send_pieces((0, 1), 2)
+    start_long(1)
+    start_long(2)
     over_heads(start_short)
+    staging[2].wait()
+    over_heads(functools.partial(send_pieces, (2,)))
+    over_heads(lambda h: pass_on(OWN, SIB, h, sibling).start())
     for copy in table:
         copy.wait()
 
@@ -317,6 +326,17 @@
             pass_on(jnp.where(my == NY - 1, VIA_M4, M2), M4, h, right).start()
             pass_on(jnp.where(my == 0, VIA_P4, P2), P4, h, left).start()
 
+        @pl.when(stage == 8)
+        def _():
+            for t in (0, 1, 2):
+                for d in (1, 2, 3):
+                    exchange(t, h, d).wait_send()
+            release(h, (SIB, M2, P2), (1, 2, 3, 4, 5), (1, 2))
+            for slot, place in ((VIA_M4, 2), (VIA_P4, 1)):
+                @pl.when(my == place)
+                def _():
+                    pass_on(OWN, slot, h, sibling).wait_send()
+
         @pl.when(stage == 9)
         def _():
             await_slot(M4, h)
@@ -325,6 +345,17 @@
         @pl.when(stage == 11)
         def _():
             await_slot(SIB2, h)
+
+    def release(h, slots, long_hops, short_hops):
+        for slot in slots:
+            pass_on(OWN, slot, h, sibling).wait_send()
+        for way in (0, 1):
+            for k in long_hops:
+                pass_long(way, k, h).wait_send()
+            for k in short_hops:
+                @pl.when(gives(way, k))
+                def _():
+                    pass_short(way, k, h).wait_send()
 
     def one_stage(stage, carry):
         hop = pick(stage, [k for _, k in STAGES])
@@ -386,22 +417,7 @@
     lax.fori_loop(0, len(STAGES), one_stage, 0)
 
     def finish(h):
-        for t in (0, 1, 2):
-            for d in (1, 2, 3):
-                exchange(t, h, d).wait_send()
-        for slot in range(M2, VIA_M4):
-            pass_on(OWN, slot, h, sibling).wait_send()
-        for slot, place in ((VIA_M4, 2), (VIA_P4, 1)):
-            @pl.when(my == place)
-            def _():
-                pass_on(OWN, slot, h, sibling).wait_send()
-        for way in (0, 1):
-            for k in range(1, 9):
-                pass_long(way, k, h).wait_send()
-            for k in range(1, 5):
-                @pl.when(gives(way, k))
-                def _():
-                    pass_short(way, k, h).wait_send()
+        release(h, (M4, P4, SIB2), (6, 7, 8), (3, 4))
         for d in (1, 2, 3):
             give_back(h, d).wait_send()
         keep_back(h).wait()
@@ -422,6 +438,7 @@
         out_specs=pl.BlockSpec(memory_space=pl.ANY),
         scratch_shapes=[
             pltpu.VMEM((SLOTS, HEADS, 2, ROWS, DIM), jnp.bfloat16),
+            pltpu.VMEM((3,) + queries.shape, jnp.bfloat16),
             pltpu.VMEM((HEADS, ROWS, DIM), jnp.bfloat16),
             pltpu.VMEM((HEADS, ROWS, DIM), jnp.bfloat16),
             pltpu.VMEM((HEADS, DIM, ROWS), jnp.float32),
@@ -432,7 +449,7 @@
             dma((3, HEADS, 3)), dma((3, HEADS, 3)), dma((3, HEADS)),
             dma((SLOTS - M2, HEADS)), dma((SLOTS - M2, HEADS)),
             dma((2, 8, HEADS)), dma((2, 8, HEADS)), dma((2, 4, HEADS)), dma((2, 4, HEADS)),
-            dma((HEADS, 3)), dma((HEADS, 3)), dma((HEADS,)), dma((2,)),
+            dma((HEADS, 3)), dma((HEADS, 3)), dma((HEADS,)), dma((5,)),
         ],
         compiler_params=pltpu.CompilerParams(
             collective_id=0, has_side_effects=True, vmem_limit_bytes=32 * 1024 * 1024

time: 71.9 us -> 71.2 us (level)
  the two profiles are of different devices: /device:TPU:40 before, /device:TPU:32 now
where the time goes in v3:
time: 71.2 us; the launch traced here: 71.1 us
  Pallas kernels  70.4 us (99%)
    pallas_call x1, Pallas kernels, local(): pl.pallas_call(kernel, out_shape=jax.ShapeDtypeStruct(queries.shape, quer...  70.4 us

profile of v3, /device:TPU:32, one launch (start us, length us, event | category | flops | bytes accessed | tf_op | source)
XLA Modules:
  0.0 71.1 jit_solution(13625696832097249377)
XLA Ops:
  0.0 70.4 %radial_attention.1 = bf16[64,1536]{1,0:T(8,128)(2,1)S(1)} custom-call(bf16[64,1536]{1,0:T(8,128)(2,1)} %q_hbm.1, bf16[64,1536]{1,0:T(8,128)(2,1)} %k_hbm.1, bf16[64,1536]{1,0:T(8,128)(2,1)} %v_hbm.1, s32[128,2,128]{2,1,0:T(2,128)} %bitcast.1, s32[128,128]{1,0:T(8,128)} %counts_hbm.1), custom_call_target="tpu_custom_call" | custom-call | tf_op jit(solution)/shard_map/radial_attention/pallas_call | solution.py:434
  70.4 0.7 copy.7

commit v4 on v3

--- a/solution.py
+++ b/solution.py
@@ -121,11 +121,6 @@
                 exchange(t, h, d).start()
             kept(t, h).start()
 
-    staging[0].wait()
-    staging[1].wait()
-    send_pieces((0, 1), 0)
-    send_pieces((0, 1), 1)
-
     def pass_on(source, slot, h, target):
         return pltpu.make_async_remote_copy(
             src_ref=kv.at[source, h],
@@ -198,25 +193,62 @@
                 for h in range(HEADS):
                     kv[slot, h, 1 - way] = jnp.zeros((ROWS, DIM), jnp.bfloat16)
 
-    def start_long(h):
+    def first_hop(way, h, t, x, source):
+        rows = pl.ds(pl.multiple_of(x * TOK, TOK), TOK)
+        send, recv = (long_send, long_recv) if t == way else (short_send, short_recv)
+        return pltpu.make_async_remote_copy(
+            src_ref=source,
+            dst_ref=held(way, 1, h, t).at[rows],
+            send_sem=send.at[way, 0, h],
+            recv_sem=recv.at[way, 0, h],
+            device_id=ways[way],
+            device_id_type=MESH,
+        )
+
+    def own_long(h):
         for way in (0, 1):
-            arrived(way, h)
-            pass_long(way, 1, h).start()
-
-    def start_short(h):
+            first_hop(way, h, way, mx, piece(way, h, mx)).start()
+
+    def own_short(h):
         for way in (0, 1):
             @pl.when(gives(way, 1))
             def _():
-                pass_short(way, 1, h).start()
-
-    start_long(0)
+                first_hop(way, h, 1 - way, mx, piece(1 - way, h, mx)).start()
+
+    def start_long(h):
+        for d in (1, 3, 2):
+            x = lax.rem(mx + NX - d, NX)
+            for way in (0, 1):
+                there = landing(way, h, x)
+                pltpu.make_async_copy(there, there, in_recv.at[way, h, d - 1]).wait()
+                first_hop(way, h, way, x, there).start()
+
+    def start_short(h):
+        for d in (1, 3, 2):
+            x = lax.rem(mx + NX - d, NX)
+            for way in (0, 1):
+                @pl.when(gives(way, 1))
+                def _():
+                    first_hop(way, h, 1 - way, x, landing(1 - way, h, x)).start()
+
+    staging[0].wait()
+    staging[1].wait()
+    send_pieces((0, 1), 0)
+    over_heads(own_long)
+    send_pieces((0, 1), 1)
     send_pieces((0, 1), 2)
-    start_long(1)
-    start_long(2)
+    over_heads(own_short)
+    over_heads(start_long)
     over_heads(start_short)
     staging[2].wait()
     over_heads(functools.partial(send_pieces, (2,)))
-    over_heads(lambda h: pass_on(OWN, SIB, h, sibling).start())
+
+    def start_sibling(h):
+        kept(0, h).wait()
+        kept(1, h).wait()
+        pass_on(OWN, SIB, h, sibling).start()
+
+    over_heads(start_sibling)
     for copy in table:
         copy.wait()
 
@@ -269,7 +301,8 @@
     zstep = NY * NC
     own_pair = ((OWN, OWN, me), (SIB, SIB, me + 1 - 2 * core))
     far = lax.rem(me + 8 * zstep, GROUPS)
-    last_pair = ((SIB2, SIB2, me - 1 + 2 * core), (BELOW + 8, ABOVE + 8, far))
+    sib2 = (SIB2, SIB2, me - 1 + 2 * core)
+    opposite = (BELOW + 8, ABOVE + 8, far)
 
     def near(k):
         return (
@@ -279,7 +312,8 @@
 
     two_pair = ((M2, M2, me - 2), (P2, P2, me + 2))
     four_pair = ((M4, M4, me - 4), (P4, P4, me + 4))
-    pairs = {0: own_pair, 4: near(1), 6: two_pair, 7: near(2), 9: four_pair, 10: near(4), 11: last_pair}
+    pairs = {0: own_pair, 4: near(1), 6: two_pair, 7: near(2), 9: four_pair, 10: near(4)}
+    singles = {8: sib2, 11: opposite}
 
     def chosen(stage, side):
         table = [pairs.get(i, own_pair)[side] for i in range(len(STAGES))]
@@ -328,6 +362,7 @@
 
         @pl.when(stage == 8)
         def _():
+            await_slot(SIB2, h)
             for t in (0, 1, 2):
                 for d in (1, 2, 3):
                     exchange(t, h, d).wait_send()
@@ -342,9 +377,6 @@
             await_slot(M4, h)
             await_slot(P4, h)
 
-        @pl.when(stage == 11)
-        def _():
-            await_slot(SIB2, h)
 
     def release(h, slots, long_hops, short_hops):
         for slot in slots:
@@ -364,6 +396,8 @@
         )
         attends = functools.reduce(jnp.logical_or, [stage == i for i in pairs])
         first, second = chosen(stage, 0), chosen(stage, 1)
+        alone = functools.reduce(jnp.logical_or, [stage == i for i in singles])
+        single = tuple(jnp.where(stage == 8, *entry) for entry in zip(sib2, opposite))
 
         def one_head(h):
             @pl.when(is_long)
@@ -379,6 +413,10 @@
             @pl.when(attends)
             def _():
                 attend(h, [first, second])
+
+            @pl.when(alone)
+            def _():
+                attend(h, [single])
 
             @pl.when(stage == len(STAGES) - 1)
             def _():

time: 71.2 us -> 70.3 us (0.987)
  Pallas kernels: 70.4 us -> 69.5 us
    pallas_call x1, Pallas kernels: 70.4 us -> 69.5 us  [local(): pl.pallas_call(kernel, out_shape=jax.ShapeDtypeStruct(queries.shape, quer...]
where the time goes in v4:
time: 70.3 us; the launch traced here: 70.2 us
  Pallas kernels  69.5 us (99%)
    pallas_call x1, Pallas kernels, local(): pl.pallas_call(kernel, out_shape=jax.ShapeDtypeStruct(queries.shape, quer...  69.5 us

profile of v4, /device:TPU:32, one launch (start us, length us, event | category | flops | bytes accessed | tf_op | source)
XLA Modules:
  0.0 70.2 jit_solution(6816268675331785983)
XLA Ops:
  0.0 69.5 %radial_attention.1 = bf16[64,1536]{1,0:T(8,128)(2,1)S(1)} custom-call(bf16[64,1536]{1,0:T(8,128)(2,1)} %q_hbm.1, bf16[64,1536]{1,0:T(8,128)(2,1)} %k_hbm.1, bf16[64,1536]{1,0:T(8,128)(2,1)} %v_hbm.1, s32[128,2,128]{2,1,0:T(2,128)} %bitcast.1, s32[128,128]{1,0:T(8,128)} %counts_hbm.1), custom_call_target="tpu_custom_call" | custom-call | tf_op jit(solution)/shard_map/radial_attention/pallas_call | solution.py:472
  69.5 0.7 copy.7

commit v5 on v4

--- a/solution.py
+++ b/solution.py
@@ -26,9 +26,20 @@
 M2, P2, M4, P4, SIB, SIB2, VIA_M4, VIA_P4 = 17, 18, 19, 20, 21, 22, 23, 24
 SLOTS = 25
 
-STAGES = (
-    ("long", 1), ("long", 2), ("long", 3), ("short", 1), ("long", 4), ("long", 5),
-    ("short", 2), ("long", 6), ("short", 3), ("long", 7), ("short", 4), ("long", 8),
+STAGES = 12
+ORDER = (
+    (
+        (3, 4, 5, 7), (3, 3, 4, 5), (2, 4, 4, 6), (2, 4, 5, 7),
+        (3, 5, 6, 7), (3, 4, 6, 7), (3, 5, 6, 7), (2, 5, 6, 7),
+        (2, 5, 5, 7), (3, 5, 6, 7), (3, 5, 6, 7), (3, 5, 6, 7),
+        (3, 5, 6, 7), (3, 5, 6, 7), (3, 5, 6, 7), (3, 5, 6, 7),
+    ),
+    (
+        (3, 4, 7, 7), (3, 5, 6, 7), (2, 5, 6, 7), (1, 4, 6, 7),
+        (3, 5, 6, 7), (2, 4, 6, 7), (3, 5, 6, 7), (2, 4, 5, 7),
+        (1, 4, 6, 7), (3, 5, 6, 7), (3, 5, 6, 7), (3, 5, 6, 7),
+        (3, 5, 6, 7), (3, 5, 6, 7), (3, 5, 6, 7), (3, 5, 6, 7),
+    ),
 )
 
 
@@ -165,25 +176,23 @@
         d = depth[way]
         return (d >= k - 1) & (d <= jnp.where(k == 3, NZ - 3, NZ - 2))
 
-    def long_hop(k, h):
-        for way in (0, 1):
-            there = held(way, k, h, way)
-            pltpu.make_async_copy(there, there, long_recv.at[way, k - 1, h]).wait()
-
-            @pl.when(k < 8)
-            def _():
-                pass_long(way, k + 1, h).start()
-
-    def short_hop(k, h):
-        for way in (0, 1):
-            @pl.when(takes(way, k))
-            def _():
-                there = held(way, k, h, 1 - way)
-                pltpu.make_async_copy(there, there, short_recv.at[way, k - 1, h]).wait()
-
-            @pl.when((k < 4) & gives(way, k + 1))
-            def _():
-                pass_short(way, k + 1, h).start()
+    def long_hop(way, k, h):
+        there = held(way, k, h, way)
+        pltpu.make_async_copy(there, there, long_recv.at[way, k - 1, h]).wait()
+
+        @pl.when(k < 8)
+        def _():
+            pass_long(way, k + 1, h).start()
+
+    def short_hop(way, k, h):
+        @pl.when(takes(way, k))
+        def _():
+            there = held(way, k, h, 1 - way)
+            pltpu.make_async_copy(there, there, short_recv.at[way, k - 1, h]).wait()
+
+        @pl.when((k < 4) & gives(way, k + 1))
+        def _():
+            pass_short(way, k + 1, h).start()
 
     for way in (0, 1):
         for k in (1, 2, 4):
@@ -316,7 +325,7 @@
     singles = {8: sib2, 11: opposite}
 
     def chosen(stage, side):
-        table = [pairs.get(i, own_pair)[side] for i in range(len(STAGES))]
+        table = [pairs.get(i, own_pair)[side] for i in range(STAGES)]
         return tuple(pick(stage, [entry[field] for entry in table]) for field in range(3))
 
     def extras(stage, h):
@@ -366,7 +375,7 @@
             for t in (0, 1, 2):
                 for d in (1, 2, 3):
                     exchange(t, h, d).wait_send()
-            release(h, (SIB, M2, P2), (1, 2, 3, 4, 5), (1, 2))
+            release(h, (SIB, M2, P2), (1, 2, 3, 4), (1,))
             for slot, place in ((VIA_M4, 2), (VIA_P4, 1)):
                 @pl.when(my == place)
                 def _():
@@ -389,24 +398,31 @@
                 def _():
                     pass_short(way, k, h).wait_send()
 
+    short_at = [
+        [pick(mz, [orders[j] + j for orders in ORDER[way]]) for j in range(4)] for way in (0, 1)
+    ]
+
     def one_stage(stage, carry):
-        hop = pick(stage, [k for _, k in STAGES])
-        is_long = functools.reduce(
-            jnp.logical_and, [stage != i for i, (kind, _) in enumerate(STAGES) if kind == "short"]
-        )
+        hops = []
+        for way in (0, 1):
+            is_short = functools.reduce(jnp.logical_or, [stage == at for at in short_at[way]])
+            short = sum(jnp.where(stage == at, j, 0) for j, at in enumerate(short_at[way], 1))
+            long = stage + 1 - sum(jnp.where(at < stage, 1, 0) for at in short_at[way])
+            hops.append((is_short, short, long))
         attends = functools.reduce(jnp.logical_or, [stage == i for i in pairs])
         first, second = chosen(stage, 0), chosen(stage, 1)
         alone = functools.reduce(jnp.logical_or, [stage == i for i in singles])
         single = tuple(jnp.where(stage == 8, *entry) for entry in zip(sib2, opposite))
 
         def one_head(h):
-            @pl.when(is_long)
-            def _():
-                long_hop(hop, h)
-
-            @pl.when(jnp.logical_not(is_long))
-            def _():
-                short_hop(hop, h)
+            for way, (is_short, short, long) in enumerate(hops):
+                @pl.when(is_short)
+                def _():
+                    short_hop(way, short, h)
+
+                @pl.when(jnp.logical_not(is_short))
+                def _():
+                    long_hop(way, long, h)
 
             extras(stage, h)
 
@@ -418,7 +434,7 @@
             def _():
                 attend(h, [single])
 
-            @pl.when(stage == len(STAGES) - 1)
+            @pl.when(stage == STAGES - 1)
             def _():
                 finish_head(h)
 
@@ -452,10 +468,10 @@
             give_back(h, d).start()
         keep_back(h).start()
 
-    lax.fori_loop(0, len(STAGES), one_stage, 0)
+    lax.fori_loop(0, STAGES, one_stage, 0)
 
     def finish(h):
-        release(h, (M4, P4, SIB2), (6, 7, 8), (3, 4))
+        release(h, (M4, P4, SIB2), (5, 6, 7, 8), (2, 3, 4))
         for d in (1, 2, 3):
             give_back(h, d).wait_send()
         keep_back(h).wait()

time: 70.3 us -> 70.5 us (level)
  the two profiles are of different devices: /device:TPU:32 before, /device:TPU:192 now
where the time goes in v5:
time: 70.5 us; the launch traced here: 70.4 us
  Pallas kernels  69.7 us (99%)
    pallas_call x1, Pallas kernels, local(): pl.pallas_call(kernel, out_shape=jax.ShapeDtypeStruct(queries.shape, quer...  69.7 us

profile of v5, /device:TPU:192, one launch (start us, length us, event | category | flops | bytes accessed | tf_op | source)
XLA Modules:
  0.0 70.4 jit_solution(14210286318343296287)
XLA Ops:
  0.0 69.7 %radial_attention.1 = bf16[64,1536]{1,0:T(8,128)(2,1)S(1)} custom-call(bf16[64,1536]{1,0:T(8,128)(2,1)} %q_hbm.1, bf16[64,1536]{1,0:T(8,128)(2,1)} %k_hbm.1, bf16[64,1536]{1,0:T(8,128)(2,1)} %v_hbm.1, s32[128,2,128]{2,1,0:T(2,128)} %bitcast.1, s32[128,128]{1,0:T(8,128)} %counts_hbm.1), custom_call_target="tpu_custom_call" | custom-call | tf_op jit(solution)/shard_map/radial_attention/pallas_call | solution.py:488
  69.7 0.7 copy.7

commit v6 on v4

--- a/solution.py
+++ b/solution.py
@@ -26,9 +26,12 @@
 M2, P2, M4, P4, SIB, SIB2, VIA_M4, VIA_P4 = 17, 18, 19, 20, 21, 22, 23, 24
 SLOTS = 25
 
+LONG = (0, 1, 2, 4, 6, 8)
+SHORT = (0, 1, 2, 4)
+
 STAGES = (
-    ("long", 1), ("long", 2), ("long", 3), ("short", 1), ("long", 4), ("long", 5),
-    ("short", 2), ("long", 6), ("short", 3), ("long", 7), ("short", 4), ("long", 8),
+    ("long", 1), ("long", 2), ("short", 1), ("long", 3), ("short", 2), ("long", 4),
+    ("none", 0), ("short", 3), ("none", 0), ("long", 5),
 )
 
 
@@ -43,7 +46,7 @@
     q_hbm, k_hbm, v_hbm, picks_hbm, counts_hbm, out_hbm,
     kv, staged, qs, os, acc, top, total, counts, picks,
     in_send, in_recv, in_local, kv_send, kv_recv, long_send, long_recv, short_send, short_recv,
-    out_send, out_recv, out_local, small_sem,
+    out_send, out_recv, out_local, small_sem, entered,
 ):
     me = lax.axis_index("frames")
     mx = lax.axis_index("heads")
@@ -54,8 +57,10 @@
     def frame(z, y, c):
         return (z * NY + y) * NC + c
 
-    up = (frame(lax.rem(mz + 1, NZ), my, core), mx)
-    down = (frame(lax.rem(mz + NZ - 1, NZ), my, core), mx)
+    def along(way, chips):
+        z = mz + chips if way == 0 else mz + NZ - chips
+        return (frame(lax.rem(z, NZ), my, core), mx)
+
     right = (frame(mz, lax.rem(my + 1, NY), core), mx)
     left = (frame(mz, lax.rem(my + NY - 1, NY), core), mx)
     sibling = (frame(mz, my, 1 - core), mx)
@@ -73,10 +78,13 @@
         copy.start()
 
     barrier = pltpu.get_barrier_semaphore()
-    partners = [up, down, right, left, sibling] + others
+    partners = [along(0, 1), along(1, 1), right, left, sibling] + others
     for partner in partners:
         pl.semaphore_signal(barrier, inc=1, device_id=partner, device_id_type=MESH)
     pl.semaphore_wait(barrier, len(partners))
+
+    for way in (0, 1):
+        pl.semaphore_signal(entered.at[way], inc=1, device_id=along(1 - way, 1), device_id_type=MESH)
 
     def landing(t, h, x):
         rows = pl.ds(pl.multiple_of(x * TOK, TOK), TOK)
@@ -135,61 +143,60 @@
         there = kv.at[slot, h]
         pltpu.make_async_copy(there, there, kv_recv.at[slot - M2, h]).wait()
 
-    ways = (up, down)
     depth = (mz, NZ - 1 - mz)
 
-    def held(way, k, h, t):
-        return kv.at[jnp.where(k == 0, OWN, (BELOW, ABOVE)[way] + k), h, t]
-
-    def pass_along(way, k, h, t, send, recv):
+    def held(way, reach, h, t):
+        return kv.at[jnp.where(reach == 0, OWN, (BELOW, ABOVE)[way] + reach), h, t]
+
+    def pass_along(way, s, h, t, reaches, send, recv):
+        start, end = pick(s, (0,) + reaches[:-1]), pick(s, reaches)
         return pltpu.make_async_remote_copy(
-            src_ref=held(way, k - 1, h, t),
-            dst_ref=held(way, k, h, t),
-            send_sem=send.at[way, k - 1, h],
-            recv_sem=recv.at[way, k - 1, h],
-            device_id=ways[way],
+            src_ref=held(way, start, h, t),
+            dst_ref=held(way, end, h, t),
+            send_sem=send.at[way, s - 1, h],
+            recv_sem=recv.at[way, s - 1, h],
+            device_id=along(way, end - start),
             device_id_type=MESH,
         )
 
-    def pass_long(way, k, h):
-        return pass_along(way, k, h, way, long_send, long_recv)
-
-    def pass_short(way, k, h):
-        return pass_along(way, k, h, 1 - way, short_send, short_recv)
-
-    def takes(way, k):
-        d = depth[way]
-        return (d >= k) & ((k != 3) | (d <= NZ - 2))
-
-    def gives(way, k):
-        d = depth[way]
-        return (d >= k - 1) & (d <= jnp.where(k == 3, NZ - 3, NZ - 2))
-
-    def long_hop(k, h):
+    def pass_long(way, s, h):
+        return pass_along(way, s, h, way, LONG, long_send, long_recv)
+
+    def pass_short(way, s, h):
+        return pass_along(way, s, h, 1 - way, SHORT, short_send, short_recv)
+
+    def takes(way, s):
+        return depth[way] >= pick(s, SHORT)
+
+    def gives(way, s):
+        start, end = pick(s, (0,) + SHORT[:-1]), pick(s, SHORT)
+        return (depth[way] >= start) & (depth[way] < NZ - (end - start))
+
+    def long_hop(s, h):
         for way in (0, 1):
-            there = held(way, k, h, way)
-            pltpu.make_async_copy(there, there, long_recv.at[way, k - 1, h]).wait()
-
-            @pl.when(k < 8)
-            def _():
-                pass_long(way, k + 1, h).start()
-
-    def short_hop(k, h):
+            there = held(way, pick(s, LONG), h, way)
+            pltpu.make_async_copy(there, there, long_recv.at[way, s - 1, h]).wait()
+
+            @pl.when(s < len(LONG) - 1)
+            def _():
+                pass_long(way, s + 1, h).start()
+
+    def short_hop(s, h):
         for way in (0, 1):
-            @pl.when(takes(way, k))
-            def _():
-                there = held(way, k, h, 1 - way)
-                pltpu.make_async_copy(there, there, short_recv.at[way, k - 1, h]).wait()
-
-            @pl.when((k < 4) & gives(way, k + 1))
-            def _():
-                pass_short(way, k + 1, h).start()
+            @pl.when(takes(way, s))
+            def _():
+                there = held(way, pick(s, SHORT), h, 1 - way)
+                pltpu.make_async_copy(there, there, short_recv.at[way, s - 1, h]).wait()
+
+            @pl.when((s < len(SHORT) - 1) & gives(way, s + 1))
+            def _():
+                pass_short(way, s + 1, h).start()
 
     for way in (0, 1):
-        for k in (1, 2, 4):
-            @pl.when(jnp.logical_not(takes(way, k)))
-            def _():
-                slot = (BELOW, ABOVE)[way] + k
+        for s, reach in enumerate(SHORT[1:], 1):
+            @pl.when(jnp.logical_not(takes(way, s)))
+            def _():
+                slot = (BELOW, ABOVE)[way] + reach
                 for h in range(HEADS):
                     kv[slot, h, 1 - way] = jnp.zeros((ROWS, DIM), jnp.bfloat16)
 
@@ -201,7 +208,7 @@
             dst_ref=held(way, 1, h, t).at[rows],
             send_sem=send.at[way, 0, h],
             recv_sem=recv.at[way, 0, h],
-            device_id=ways[way],
+            device_id=along(way, 1),
             device_id_type=MESH,
         )
 
@@ -249,6 +256,8 @@
         pass_on(OWN, SIB, h, sibling).start()
 
     over_heads(start_sibling)
+    for way in (0, 1):
+        pl.semaphore_wait(entered.at[way], 1)
     for copy in table:
         copy.wait()
 
@@ -312,8 +321,8 @@
 
     two_pair = ((M2, M2, me - 2), (P2, P2, me + 2))
     four_pair = ((M4, M4, me - 4), (P4, P4, me + 4))
-    pairs = {0: own_pair, 4: near(1), 6: two_pair, 7: near(2), 9: four_pair, 10: near(4)}
-    singles = {8: sib2, 11: opposite}
+    pairs = {0: own_pair, 2: near(1), 4: two_pair, 5: near(2), 6: four_pair, 7: near(4)}
+    singles = {8: sib2, 9: opposite}
 
     def chosen(stage, side):
         table = [pairs.get(i, own_pair)[side] for i in range(len(STAGES))]
@@ -325,30 +334,28 @@
             arrived(2, h)
             await_slot(SIB, h)
 
-        @pl.when(((stage == 0) & (my < NY - 1)) | ((stage == 3) & (my == NY - 1)))
+        @pl.when(((stage == 0) & (my < NY - 1)) | ((stage == 2) & (my == NY - 1)))
         def _():
             pass_on(jnp.where(my == NY - 1, BELOW + 1, OWN), M2, h, right).start()
 
-        @pl.when(((stage == 1) & (my > 0)) | ((stage == 3) & (my == 0)))
+        @pl.when(((stage == 1) & (my > 0)) | ((stage == 2) & (my == 0)))
         def _():
             pass_on(jnp.where(my == 0, ABOVE + 1, OWN), P2, h, left).start()
 
-        @pl.when((stage == 3) & (my == 2))
+        @pl.when((stage == 2) & (my == 2))
         def _():
             pass_on(BELOW + 1, VIA_M4, h, right).start()
 
-        @pl.when((stage == 3) & (my == 1))
+        @pl.when((stage == 2) & (my == 1))
         def _():
             pass_on(ABOVE + 1, VIA_P4, h, left).start()
 
-        @pl.when(stage == 6)
+        @pl.when(stage == 4)
         def _():
             await_slot(M2, h)
             await_slot(P2, h)
             pass_on(jnp.where(core == 1, M2, P2), SIB2, h, sibling).start()
 
-        @pl.when(stage == 7)
-        def _():
             @pl.when(my == NY - 1)
             def _():
                 await_slot(VIA_M4, h)
@@ -366,13 +373,13 @@
             for t in (0, 1, 2):
                 for d in (1, 2, 3):
                     exchange(t, h, d).wait_send()
-            release(h, (SIB, M2, P2), (1, 2, 3, 4, 5), (1, 2))
+            release(h, (SIB, M2, P2), (1, 2, 3), (1, 2))
             for slot, place in ((VIA_M4, 2), (VIA_P4, 1)):
                 @pl.when(my == place)
                 def _():
                     pass_on(OWN, slot, h, sibling).wait_send()
 
-        @pl.when(stage == 9)
+        @pl.when(stage == 6)
         def _():
             await_slot(M4, h)
             await_slot(P4, h)
@@ -392,7 +399,10 @@
     def one_stage(stage, carry):
         hop = pick(stage, [k for _, k in STAGES])
         is_long = functools.reduce(
-            jnp.logical_and, [stage != i for i, (kind, _) in enumerate(STAGES) if kind == "short"]
+            jnp.logical_or, [stage == i for i, (kind, _) in enumerate(STAGES) if kind == "long"]
+        )
+        is_short = functools.reduce(
+            jnp.logical_or, [stage == i for i, (kind, _) in enumerate(STAGES) if kind == "short"]
         )
         attends = functools.reduce(jnp.logical_or, [stage == i for i in pairs])
         first, second = chosen(stage, 0), chosen(stage, 1)
@@ -404,7 +414,7 @@
             def _():
                 long_hop(hop, h)
 
-            @pl.when(jnp.logical_not(is_long))
+            @pl.when(is_short)
             def _():
                 short_hop(hop, h)
 
@@ -455,7 +465,7 @@
     lax.fori_loop(0, len(STAGES), one_stage, 0)
 
     def finish(h):
-        release(h, (M4, P4, SIB2), (6, 7, 8), (3, 4))
+        release(h, (M4, P4, SIB2), (4, 5), (3,))
         for d in (1, 2, 3):
             give_back(h, d).wait_send()
         keep_back(h).wait()
@@ -486,8 +496,8 @@
             pltpu.SMEM((2, GROUPS), jnp.int32),
             dma((3, HEADS, 3)), dma((3, HEADS, 3)), dma((3, HEADS)),
             dma((SLOTS - M2, HEADS)), dma((SLOTS - M2, HEADS)),
-            dma((2, 8, HEADS)), dma((2, 8, HEADS)), dma((2, 4, HEADS)), dma((2, 4, HEADS)),
-            dma((HEADS, 3)), dma((HEADS, 3)), dma((HEADS,)), dma((5,)),
+            dma((2, 5, HEADS)), dma((2, 5, HEADS)), dma((2, 3, HEADS)), dma((2, 3, HEADS)),
+            dma((HEADS, 3)), dma((HEADS, 3)), dma((HEADS,)), dma((5,)), pltpu.SemaphoreType.REGULAR((2,)),
         ],
         compiler_params=pltpu.CompilerParams(
             collective_id=0, has_side_effects=True, vmem_limit_bytes=32 * 1024 * 1024

time: 70.3 us -> 69.2 us (0.984)
  the two profiles are of different devices: /device:TPU:32 before, /device:TPU:192 now
where the time goes in v6:
time: 69.2 us; the launch traced here: 69.1 us
  Pallas kernels  68.4 us (99%)
    pallas_call x1, Pallas kernels, local(): pl.pallas_call(kernel, out_shape=jax.ShapeDtypeStruct(queries.shape, quer...  68.4 us

profile of v6, /device:TPU:192, one launch (start us, length us, event | category | flops | bytes accessed | tf_op | source)
XLA Modules:
  0.0 69.1 jit_solution(7093088044136370465)
XLA Ops:
  0.0 68.4 %radial_attention.1 = bf16[64,1536]{1,0:T(8,128)(2,1)S(1)} custom-call(bf16[64,1536]{1,0:T(8,128)(2,1)} %q_hbm.1, bf16[64,1536]{1,0:T(8,128)(2,1)} %k_hbm.1, bf16[64,1536]{1,0:T(8,128)(2,1)} %v_hbm.1, s32[128,2,128]{2,1,0:T(2,128)} %bitcast.1, s32[128,128]{1,0:T(8,128)} %counts_hbm.1), custom_call_target="tpu_custom_call" | custom-call | tf_op jit(solution)/shard_map/radial_attention/pallas_call | solution.py:482
  68.4 0.7 copy.7

commit v7 on v6

--- a/solution.py
+++ b/solution.py
@@ -26,13 +26,20 @@
 M2, P2, M4, P4, SIB, SIB2, VIA_M4, VIA_P4 = 17, 18, 19, 20, 21, 22, 23, 24
 SLOTS = 25
 
-LONG = (0, 1, 2, 4, 6, 8)
-SHORT = (0, 1, 2, 4)
+LONG = ((0, 1, 2, 4, 6, 8), (0, 1, 2, 3, 4, 5, 6, 7, 8))
+SHORT = ((0, 1, 2, 4), (0, 1, 2, 3, 4))
 
 STAGES = (
-    ("long", 1), ("long", 2), ("short", 1), ("long", 3), ("short", 2), ("long", 4),
-    ("none", 0), ("short", 3), ("none", 0), ("long", 5),
+    (
+        ("long", 1), ("long", 2), ("short", 1), ("long", 3), ("short", 2), ("long", 4),
+        ("none", 0), ("short", 3), ("none", 0), ("long", 5), ("none", 0), ("none", 0),
+    ),
+    (
+        ("long", 1), ("long", 2), ("long", 3), ("short", 1), ("long", 4), ("long", 5),
+        ("short", 2), ("long", 6), ("short", 3), ("long", 7), ("short", 4), ("long", 8),
+    ),
 )
+COUNT = 12
 
 
 def pick(index, values):
@@ -148,8 +155,16 @@
     def held(way, reach, h, t):
         return kv.at[jnp.where(reach == 0, OWN, (BELOW, ABOVE)[way] + reach), h, t]
 
+    def by_core(zero, one):
+        return jnp.where(core == 0, zero, one)
+
+    def reach_of(s, reaches):
+        return by_core(pick(s, reaches[0]), pick(s, reaches[1]))
+
+    last_long, last_short = (by_core(len(r[0]) - 1, len(r[1]) - 1) for r in (LONG, SHORT))
+
     def pass_along(way, s, h, t, reaches, send, recv):
-        start, end = pick(s, (0,) + reaches[:-1]), pick(s, reaches)
+        start, end = reach_of(s - 1, reaches), reach_of(s, reaches)
         return pltpu.make_async_remote_copy(
             src_ref=held(way, start, h, t),
             dst_ref=held(way, end, h, t),
@@ -166,18 +181,19 @@
         return pass_along(way, s, h, 1 - way, SHORT, short_send, short_recv)
 
     def takes(way, s):
-        return depth[way] >= pick(s, SHORT)
+        d, reach = depth[way], reach_of(s, SHORT)
+        return (s <= last_short) & (d >= reach) & ((reach != 3) | (d < NZ - 1))
 
     def gives(way, s):
-        start, end = pick(s, (0,) + SHORT[:-1]), pick(s, SHORT)
-        return (depth[way] >= start) & (depth[way] < NZ - (end - start))
+        d, start, end = depth[way], reach_of(s - 1, SHORT), reach_of(s, SHORT)
+        return (s <= last_short) & (d >= start) & (d < NZ - (end - start) - jnp.where(end == 3, 1, 0))
 
     def long_hop(s, h):
         for way in (0, 1):
-            there = held(way, pick(s, LONG), h, way)
+            there = held(way, reach_of(s, LONG), h, way)
             pltpu.make_async_copy(there, there, long_recv.at[way, s - 1, h]).wait()
 
-            @pl.when(s < len(LONG) - 1)
+            @pl.when(s < last_long)
             def _():
                 pass_long(way, s + 1, h).start()
 
@@ -185,16 +201,16 @@
         for way in (0, 1):
             @pl.when(takes(way, s))
             def _():
-                there = held(way, pick(s, SHORT), h, 1 - way)
+                there = held(way, reach_of(s, SHORT), h, 1 - way)
                 pltpu.make_async_copy(there, there, short_recv.at[way, s - 1, h]).wait()
 
-            @pl.when((s < len(SHORT) - 1) & gives(way, s + 1))
+            @pl.when(gives(way, s + 1))
             def _():
                 pass_short(way, s + 1, h).start()
 
     for way in (0, 1):
-        for s, reach in enumerate(SHORT[1:], 1):
-            @pl.when(jnp.logical_not(takes(way, s)))
+        for reach in (1, 2, 4):
+            @pl.when(depth[way] < reach)
             def _():
                 slot = (BELOW, ABOVE)[way] + reach
                 for h in range(HEADS):
@@ -321,12 +337,19 @@
 
     two_pair = ((M2, M2, me - 2), (P2, P2, me + 2))
     four_pair = ((M4, M4, me - 4), (P4, P4, me + 4))
-    pairs = {0: own_pair, 2: near(1), 4: two_pair, 5: near(2), 6: four_pair, 7: near(4)}
-    singles = {8: sib2, 9: opposite}
+    pairs = [
+        (by_core(*at), pair) for at, pair in (
+            ((0, 0), own_pair), ((2, 4), near(1)), ((4, 6), two_pair),
+            ((5, 7), near(2)), ((6, 9), four_pair), ((7, 10), near(4)),
+        )
+    ]
+    far_stage = by_core(9, 11)
 
     def chosen(stage, side):
-        table = [pairs.get(i, own_pair)[side] for i in range(len(STAGES))]
-        return tuple(pick(stage, [entry[field] for entry in table]) for field in range(3))
+        found = own_pair[side]
+        for at, pair in pairs[1:]:
+            found = tuple(jnp.where(stage == at, new, old) for new, old in zip(pair[side], found))
+        return found
 
     def extras(stage, h):
         @pl.when(stage == 0)
@@ -334,23 +357,23 @@
             arrived(2, h)
             await_slot(SIB, h)
 
-        @pl.when(((stage == 0) & (my < NY - 1)) | ((stage == 2) & (my == NY - 1)))
+        @pl.when(((stage == 0) & (my < NY - 1)) | ((stage == by_core(2, 3)) & (my == NY - 1)))
         def _():
             pass_on(jnp.where(my == NY - 1, BELOW + 1, OWN), M2, h, right).start()
 
-        @pl.when(((stage == 1) & (my > 0)) | ((stage == 2) & (my == 0)))
+        @pl.when(((stage == 1) & (my > 0)) | ((stage == by_core(2, 3)) & (my == 0)))
         def _():
             pass_on(jnp.where(my == 0, ABOVE + 1, OWN), P2, h, left).start()
 
-        @pl.when((stage == 2) & (my == 2))
+        @pl.when((stage == by_core(2, 3)) & (my == 2))
         def _():
             pass_on(BELOW + 1, VIA_M4, h, right).start()
 
-        @pl.when((stage == 2) & (my == 1))
+        @pl.when((stage == by_core(2, 3)) & (my == 1))
         def _():
             pass_on(ABOVE + 1, VIA_P4, h, left).start()
 
-        @pl.when(stage == 4)
+        @pl.when(stage == by_core(4, 6))
         def _():
             await_slot(M2, h)
             await_slot(P2, h)
@@ -379,7 +402,7 @@
                 def _():
                     pass_on(OWN, slot, h, sibling).wait_send()
 
-        @pl.when(stage == 6)
+        @pl.when(stage == by_core(6, 9))
         def _():
             await_slot(M4, h)
             await_slot(P4, h)
@@ -390,23 +413,29 @@
             pass_on(OWN, slot, h, sibling).wait_send()
         for way in (0, 1):
             for k in long_hops:
-                pass_long(way, k, h).wait_send()
+                @pl.when(k <= last_long)
+                def _():
+                    pass_long(way, k, h).wait_send()
+
             for k in short_hops:
                 @pl.when(gives(way, k))
                 def _():
                     pass_short(way, k, h).wait_send()
 
     def one_stage(stage, carry):
-        hop = pick(stage, [k for _, k in STAGES])
-        is_long = functools.reduce(
-            jnp.logical_or, [stage == i for i, (kind, _) in enumerate(STAGES) if kind == "long"]
-        )
-        is_short = functools.reduce(
-            jnp.logical_or, [stage == i for i, (kind, _) in enumerate(STAGES) if kind == "short"]
-        )
-        attends = functools.reduce(jnp.logical_or, [stage == i for i in pairs])
+        def is_kind(name):
+            return by_core(*(
+                functools.reduce(
+                    jnp.logical_or, [stage == i for i, (kind, _) in enumerate(stages) if kind == name]
+                )
+                for stages in STAGES
+            ))
+
+        hop = by_core(*(pick(stage, [s for _, s in stages]) for stages in STAGES))
+        is_long, is_short = is_kind("long"), is_kind("short")
+        attends = functools.reduce(jnp.logical_or, [stage == at for at, _ in pairs])
         first, second = chosen(stage, 0), chosen(stage, 1)
-        alone = functools.reduce(jnp.logical_or, [stage == i for i in singles])
+        alone = (stage == 8) | (stage == far_stage)
         single = tuple(jnp.where(stage == 8, *entry) for entry in zip(sib2, opposite))
 
         def one_head(h):
@@ -428,7 +457,7 @@
             def _():
                 attend(h, [single])
 
-            @pl.when(stage == len(STAGES) - 1)
+            @pl.when(stage == far_stage)
             def _():
                 finish_head(h)
 
@@ -462,10 +491,10 @@
             give_back(h, d).start()
         keep_back(h).start()
 
-    lax.fori_loop(0, len(STAGES), one_stage, 0)
+    lax.fori_loop(0, COUNT, one_stage, 0)
 
     def finish(h):
-        release(h, (M4, P4, SIB2), (4, 5), (3,))
+        release(h, (M4, P4, SIB2), (4, 5, 6, 7, 8), (3, 4))
         for d in (1, 2, 3):
             give_back(h, d).wait_send()
         keep_back(h).wait()
@@ -496,7 +525,7 @@
             pltpu.SMEM((2, GROUPS), jnp.int32),
             dma((3, HEADS, 3)), dma((3, HEADS, 3)), dma((3, HEADS)),
             dma((SLOTS - M2, HEADS)), dma((SLOTS - M2, HEADS)),
-            dma((2, 5, HEADS)), dma((2, 5, HEADS)), dma((2, 3, HEADS)), dma((2, 3, HEADS)),
+            dma((2, 8, HEADS)), dma((2, 8, HEADS)), dma((2, 4, HEADS)), dma((2, 4, HEADS)),
             dma((HEADS, 3)), dma((HEADS, 3)), dma((HEADS,)), dma((5,)), pltpu.SemaphoreType.REGULAR((2,)),
         ],
         compiler_params=pltpu.CompilerParams(

time: 69.2 us -> 70 us (1.012)
  the two profiles are of different devices: /device:TPU:192 before, /device:TPU:1 now
where the time goes in v7:
time: 70 us; the launch traced here: 69.9 us
  Pallas kernels  69.2 us (99%)
    pallas_call x1, Pallas kernels, local(): pl.pallas_call(kernel, out_shape=jax.ShapeDtypeStruct(queries.shape, quer...  69.2 us

profile of v7, /device:TPU:1, one launch (start us, length us, event | category | flops | bytes accessed | tf_op | source)
XLA Modules:
  0.0 69.9 jit_solution(10378771546495406442)
XLA Ops:
  0.0 69.2 %radial_attention.1 = bf16[64,1536]{1,0:T(8,128)(2,1)S(1)} custom-call(bf16[64,1536]{1,0:T(8,128)(2,1)} %q_hbm.1, bf16[64,1536]{1,0:T(8,128)(2,1)} %k_hbm.1, bf16[64,1536]{1,0:T(8,128)(2,1)} %v_hbm.1, s32[128,2,128]{2,1,0:T(2,128)} %bitcast.1, s32[128,128]{1,0:T(8,128)} %counts_hbm.1), custom_call_target="tpu_custom_call" | custom-call | tf_op jit(solution)/shard_map/radial_attention/pallas_call | solution.py:511
  69.2 0.7 copy.7

commit v8 on v7

--- a/solution.py
+++ b/solution.py
@@ -26,13 +26,13 @@
 M2, P2, M4, P4, SIB, SIB2, VIA_M4, VIA_P4 = 17, 18, 19, 20, 21, 22, 23, 24
 SLOTS = 25
 
-LONG = ((0, 1, 2, 4, 6, 8), (0, 1, 2, 3, 4, 5, 6, 7, 8))
+LONG = ((0, 1, 2, 3, 4, 6, 8), (0, 1, 2, 3, 4, 5, 6, 7, 8))
 SHORT = ((0, 1, 2, 4), (0, 1, 2, 3, 4))
 
 STAGES = (
     (
-        ("long", 1), ("long", 2), ("short", 1), ("long", 3), ("short", 2), ("long", 4),
-        ("none", 0), ("short", 3), ("none", 0), ("long", 5), ("none", 0), ("none", 0),
+        ("long", 1), ("long", 2), ("long", 3), ("short", 1), ("long", 4), ("short", 2),
+        ("long", 5), ("none", 0), ("short", 3), ("none", 0), ("long", 6), ("none", 0),
     ),
     (
         ("long", 1), ("long", 2), ("long", 3), ("short", 1), ("long", 4), ("long", 5),
@@ -339,11 +339,11 @@
     four_pair = ((M4, M4, me - 4), (P4, P4, me + 4))
     pairs = [
         (by_core(*at), pair) for at, pair in (
-            ((0, 0), own_pair), ((2, 4), near(1)), ((4, 6), two_pair),
-            ((5, 7), near(2)), ((6, 9), four_pair), ((7, 10), near(4)),
+            ((0, 0), own_pair), ((3, 4), near(1)), ((5, 6), two_pair),
+            ((6, 7), near(2)), ((7, 9), four_pair), ((8, 10), near(4)),
         )
     ]
-    far_stage = by_core(9, 11)
+    far_stage = by_core(10, 11)
 
     def chosen(stage, side):
         found = own_pair[side]
@@ -357,23 +357,23 @@
             arrived(2, h)
             await_slot(SIB, h)
 
-        @pl.when(((stage == 0) & (my < NY - 1)) | ((stage == by_core(2, 3)) & (my == NY - 1)))
+        @pl.when(((stage == 0) & (my < NY - 1)) | ((stage == 3) & (my == NY - 1)))
         def _():
             pass_on(jnp.where(my == NY - 1, BELOW + 1, OWN), M2, h, right).start()
 
-        @pl.when(((stage == 1) & (my > 0)) | ((stage == by_core(2, 3)) & (my == 0)))
+        @pl.when(((stage == 1) & (my > 0)) | ((stage == 3) & (my == 0)))
         def _():
             pass_on(jnp.where(my == 0, ABOVE + 1, OWN), P2, h, left).start()
 
-        @pl.when((stage == by_core(2, 3)) & (my == 2))
+        @pl.when((stage == 3) & (my == 2))
         def _():
             pass_on(BELOW + 1, VIA_M4, h, right).start()
 
-        @pl.when((stage == by_core(2, 3)) & (my == 1))
+        @pl.when((stage == 3) & (my == 1))
         def _():
             pass_on(ABOVE + 1, VIA_P4, h, left).start()
 
-        @pl.when(stage == by_core(4, 6))
+        @pl.when(stage == by_core(5, 6))
         def _():
             await_slot(M2, h)
             await_slot(P2, h)
@@ -402,7 +402,7 @@
                 def _():
                     pass_on(OWN, slot, h, sibling).wait_send()
 
-        @pl.when(stage == by_core(6, 9))
+        @pl.when(stage == by_core(7, 9))
         def _():
             await_slot(M4, h)
             await_slot(P4, h)

time: 70 us -> 70 us (level)
  no operation moved by 1% of the time
where the time goes in v8:
time: 70 us; the launch traced here: 69.5 us
  Pallas kernels  68.8 us (98%)
    pallas_call x1, Pallas kernels, local(): pl.pallas_call(kernel, out_shape=jax.ShapeDtypeStruct(queries.shape, quer...  68.8 us

profile of v8, /device:TPU:1, one launch (start us, length us, event | category | flops | bytes accessed | tf_op | source)
XLA Modules:
  0.0 69.5 jit_solution(3752367766156232523)
XLA Ops:
  0.0 68.8 %radial_attention.1 = bf16[64,1536]{1,0:T(8,128)(2,1)S(1)} custom-call(bf16[64,1536]{1,0:T(8,128)(2,1)} %q_hbm.1, bf16[64,1536]{1,0:T(8,128)(2,1)} %k_hbm.1, bf16[64,1536]{1,0:T(8,128)(2,1)} %v_hbm.1, s32[128,2,128]{2,1,0:T(2,128)} %bitcast.1, s32[128,128]{1,0:T(8,128)} %counts_hbm.1), custom_call_target="tpu_custom_call" | custom-call | tf_op jit(solution)/shard_map/radial_attention/pallas_call | solution.py:511
  68.8 0.7 copy.7

commit v9 on v7

--- a/solution.py
+++ b/solution.py
@@ -26,7 +26,7 @@
 M2, P2, M4, P4, SIB, SIB2, VIA_M4, VIA_P4 = 17, 18, 19, 20, 21, 22, 23, 24
 SLOTS = 25
 
-LONG = ((0, 1, 2, 4, 6, 8), (0, 1, 2, 3, 4, 5, 6, 7, 8))
+LONG = ((0, 1, 2, 4, 6, 8), (0, 1, 2, 3, 4, 5, 6, 8))
 SHORT = ((0, 1, 2, 4), (0, 1, 2, 3, 4))
 
 STAGES = (
@@ -36,7 +36,7 @@
     ),
     (
         ("long", 1), ("long", 2), ("long", 3), ("short", 1), ("long", 4), ("long", 5),
-        ("short", 2), ("long", 6), ("short", 3), ("long", 7), ("short", 4), ("long", 8),
+        ("short", 2), ("long", 6), ("short", 3), ("none", 0), ("short", 4), ("long", 7),
     ),
 )
 COUNT = 12

time: 70 us -> 70.3 us (level)
  no operation moved by 1% of the time
where the time goes in v9:
time: 70.3 us; the launch traced here: 69.7 us
  Pallas kernels  69.1 us (98%)
    pallas_call x1, Pallas kernels, local(): pl.pallas_call(kernel, out_shape=jax.ShapeDtypeStruct(queries.shape, quer...  69.1 us

profile of v9, /device:TPU:1, one launch (start us, length us, event | category | flops | bytes accessed | tf_op | source)
XLA Modules:
  0.0 69.7 jit_solution(6334995527398250782)
XLA Ops:
  0.0 69.1 %radial_attention.1 = bf16[64,1536]{1,0:T(8,128)(2,1)S(1)} custom-call(bf16[64,1536]{1,0:T(8,128)(2,1)} %q_hbm.1, bf16[64,1536]{1,0:T(8,128)(2,1)} %k_hbm.1, bf16[64,1536]{1,0:T(8,128)(2,1)} %v_hbm.1, s32[128,2,128]{2,1,0:T(2,128)} %bitcast.1, s32[128,128]{1,0:T(8,128)} %counts_hbm.1), custom_call_target="tpu_custom_call" | custom-call | tf_op jit(solution)/shard_map/radial_attention/pallas_call | solution.py:511
  69.1 0.7 copy.7
